TPU v7x, 256 devices: a whole 4x4x8 slice. The times are simulated.
256 devices in a mesh: shard: 32 (over y, z_lo, core), rep: 8 (over x, z_hi).
Axes of the slice: x: 4, y: 4, z: 8 (z_hi: 2, z_lo: 4; z = z_hi * 4 + z_lo), core: 2. Of those that a mesh axis runs over, the one named last changes fastest.
Arguments:
- table: float32 [524288, 256], P(('shard', 'rep')), may hold values from -6 to 6
- swap_mask: int32 [8], P('rep'), may hold values from 1 to 31
- swap_slots: int32 [256, 8], P(('shard', 'rep')), may hold values from 0 to 15, as said below
- hot_ids: int32 [32, 4], P('shard'), may hold values from 0 to 127, as said below
- req_idx: int32 [32, 2048, 16], P('shard'), may hold values from 0 to 16383
- req_count: int32 [32, 2048], P('shard'), may hold values from 1 to 16
Outputs:
- table_after: float32 [524288, 256], P(('shard', 'rep'))
- hot_cache: float32 [32, 512, 256], P('shard')
- pooled: float32 [32, 2048, 256], P('shard', 'rep')
Inputs may be any that keep to these rules, and one draw needn't show every extreme that they name: `swap_slots`: the entries of a row are distinct local block numbers. `hot_ids`: the entries of a row are distinct block numbers of the group.
All inputs are finite; a program needn't handle non-finite values.
Results may differ from a plain program's by a relative error of at most 0.0003.
Values sent between devices are 32-bit elements; how exact they have to be, the bound alone decides.
No kernel may reach another device: no remote copies, remote signals or barrier semaphores. Data moves between devices by JAX's collectives and lax.ppermute only.
A program may use at most 64 MiB of HBM per device.

v0:
```python
import functools

import jax
import jax.numpy as jnp
from jax import lax
from jax.experimental import pallas as pl
from jax.experimental.pallas import tpu as pltpu
from jax.sharding import PartitionSpec as P

BLOCK = 128
E = 256
BLK_DEV = 16
SWAPS = 8
HOT = 4
K = 16
N_SHARD = 32
N_X = 4
N_REP = 8
OWN = 256
REQS = OWN * N_REP
PIECES = 8
HALF_ROWS = SWAPS * BLOCK
CHUNKS = 4
WIDE = E // CHUNKS
COUNT_INT = jnp.int16

SMEM = pl.BlockSpec(memory_space=pltpu.SMEM)
VMEM = pl.BlockSpec(memory_space=pltpu.VMEM)
ANY = pl.BlockSpec(memory_space=pl.ANY)


def f32(*shape):
    return jax.ShapeDtypeStruct(shape, jnp.float32)


def params(mib):
    return pltpu.CompilerParams(vmem_limit_bytes=mib * 2**20)


def cost(flops, moved):
    return pl.CostEstimate(flops=flops, bytes_accessed=moved, transcendentals=0)


def piece_owner(piece, rep):
    ahead = piece % N_X
    side = 1 - piece // N_X
    x = lax.rem(rep // 2 + ahead, N_X)
    return x * 2 + lax.rem(lax.rem(rep, 2) + side, 2)


def outgoing_kernel(slots, table, out, sems):
    copies = [
        pltpu.make_async_copy(table.at[slots[0, j]], out.at[j], sems.at[j]) for j in range(SWAPS)
    ]
    for copy in copies:
        copy.start()
    for copy in copies:
        copy.wait()


def outgoing(slots, blocks):
    return pl.pallas_call(
        outgoing_kernel,
        out_shape=f32(SWAPS, BLOCK, E),
        in_specs=[SMEM, ANY],
        out_specs=ANY,
        scratch_shapes=[pltpu.SemaphoreType.DMA((SWAPS,))],
        cost_estimate=cost(0, 2**21),
    )(slots, blocks)


def early_kernel(slots, hot, raw_keys, counts, table, sums, later, keys, flags, order, parts):
    rep = lax.axis_index("rep")

    def clear(b, carry):
        flags[b] = 0
        return carry

    def mark(j, carry):
        flags[slots[0, j]] = 1
        order[SWAPS + j] = slots[0, j]
        return carry

    def list_block(b, found):
        @pl.when(flags[b] == 0)
        def _():
            order[found] = b

        return found + 1 - flags[b]

    lax.fori_loop(0, BLK_DEV, clear, 0)
    lax.fori_loop(0, SWAPS, mark, 0)
    lax.fori_loop(0, BLK_DEV, list_block, 0)
    live = lax.broadcasted_iota(jnp.int32, (K, REQS), 0) < counts[...]
    keys[...] = jnp.where(live, raw_keys[...], -1)

    def split(j, carry):
        put_parts(table[order[j]], j, parts)
        return carry

    lax.fori_loop(0, SWAPS, split, 0)
    row_in_tile = lax.broadcasted_iota(jnp.int32, (16, 128), 0).astype(COUNT_INT)
    one, zero = jnp.bfloat16(1), jnp.bfloat16(0)

    def one_piece(piece, carry):
        start = piece_owner(piece, rep) * OWN

        def one_block(step, inner):
            j = step // 2
            side = step % 2 * 128
            lanes = pl.multiple_of(start + side, 128)
            column = pl.multiple_of(side, 128)
            place = jnp.where(j < SWAPS, PIECES, piece)
            first = (rep * BLK_DEV + order[j]) * BLOCK
            near = []
            for k in range(K):
                offset = jnp.clip(keys[pl.ds(k, 1), pl.ds(lanes, 128)] - first, -1, BLOCK)
                near.append(jnp.broadcast_to(offset, (16, 128)).astype(COUNT_INT))
            for tile in range(BLOCK // 16):
                row = row_in_tile + jnp.array(tile * 16, COUNT_INT)
                total = jnp.where(near[0] == row, one, zero)
                for k in range(1, K):
                    total = total + jnp.where(near[k] == row, one, zero)
                row0 = pl.multiple_of(j % SWAPS * BLOCK + tile * 16, 16)
                later[place, pl.ds(row0, 16), pl.ds(column, 128)] = total
            return inner

        lax.fori_loop(0, BLK_DEV * 2, one_block, 0)
        apply_counts(parts, later.at[PIECES], sums.at[piece])
        return carry

    lax.fori_loop(0, PIECES, one_piece, 0)


def turn_rows(rows):
    turned = rows.T
    high = turned.astype(jnp.bfloat16)
    return high, (turned - high.astype(jnp.float32)).astype(jnp.bfloat16)


def put_parts(rows, j, parts):
    high, low = turn_rows(rows)
    at = pl.ds(pl.multiple_of(j * BLOCK, BLOCK), BLOCK)
    for chunk in range(CHUNKS):
        parts[chunk, :WIDE, at] = high[chunk * WIDE : (chunk + 1) * WIDE]
        parts[chunk, WIDE:, at] = low[chunk * WIDE : (chunk + 1) * WIDE]


def apply_counts(parts, counted, out):
    def one_chunk(chunk, carry):
        both = jnp.dot(parts[chunk], counted[...], preferred_element_type=jnp.float32)
        out[pl.ds(pl.multiple_of(chunk * WIDE, WIDE), WIDE)] = both[:WIDE] + both[WIDE:]
        return carry

    lax.fori_loop(0, CHUNKS, one_chunk, 0)


def early(slots, hot, keys, counts, blocks):
    return pl.pallas_call(
        early_kernel,
        out_shape=(
            f32(PIECES, E, OWN),
            jax.ShapeDtypeStruct((PIECES + 1, HALF_ROWS, OWN), jnp.bfloat16),
        ),
        in_specs=[SMEM, SMEM, VMEM, VMEM, VMEM],
        out_specs=(VMEM, VMEM),
        scratch_shapes=[
            pltpu.VMEM((K, REQS), jnp.int32),
            pltpu.SMEM((BLK_DEV,), jnp.int32),
            pltpu.SMEM((BLK_DEV,), jnp.int32),
            pltpu.VMEM((CHUNKS, 2 * WIDE, HALF_ROWS), jnp.bfloat16),
        ],
        compiler_params=params(16),
        cost_estimate=cost(2**34, 2**25),
    )(slots, hot, keys, counts, blocks)


def late_kernel(sums, later, incoming, out0, out1, out2, out3, parts):
    for j in range(SWAPS):
        high, low = turn_rows(incoming[j])
        parts[:E, j * BLOCK : (j + 1) * BLOCK] = high
        parts[E:, j * BLOCK : (j + 1) * BLOCK] = low
    for ahead, out in ((2, out2), (1, out1), (3, out3), (0, out0)):
        both = jnp.dot(parts[...], later[ahead], preferred_element_type=jnp.float32)
        out[...] = sums[ahead] + both[:E] + both[E:]


def late(sums, later, incoming):
    return pl.pallas_call(
        late_kernel,
        out_shape=(f32(E, OWN),) * N_X + (jax.ShapeDtypeStruct((2 * E, HALF_ROWS), jnp.bfloat16),),
        in_specs=[VMEM] * 3,
        out_specs=(VMEM,) * (N_X + 1),
        compiler_params=params(16),
        cost_estimate=cost(2**30, 2**22),
    )(sums, later, incoming)


def home_kernel(sums, later, parts, out0, out1, out2, out3):
    for ahead, out in ((2, out2), (1, out1), (3, out3), (0, out0)):
        both = jnp.dot(parts[...], later[N_X + ahead], preferred_element_type=jnp.float32)
        out[:E] = sums[N_X + ahead] + both[:E] + both[E:]


def home(sums, later, parts):
    return pl.pallas_call(
        home_kernel,
        out_shape=(f32(E, OWN),) + (f32(E + BLOCK, OWN),) * (N_X - 1),
        in_specs=[VMEM] * 3,
        out_specs=(VMEM,) * N_X,
        compiler_params=params(16),
        cost_estimate=cost(2**30, 2**22),
    )(sums, later, parts)


def add_hot_kernel(hot, mine, other, in1, in2, in3, out1, out2, out3, hot_out, sems):
    rep = lax.axis_index("rep")
    side = lax.rem(hot[0, rep // 2] // BLK_DEV, 2)

    @pl.when(side == lax.rem(rep, 2))
    def _():
        hot_out[...] = mine[...]

    @pl.when(side != lax.rem(rep, 2))
    def _():
        hot_out[...] = other[...]

    copies = [
        pltpu.make_async_copy(hot_out, out.at[pl.ds(E, BLOCK)], sems.at[n])
        for n, out in enumerate((out1, out2, out3))
    ]
    for copy in copies:
        copy.start()
    for copy in copies:
        copy.wait()


def add_hot(hot, mine, other, homeward):
    return pl.pallas_call(
        add_hot_kernel,
        out_shape=(f32(E + BLOCK, OWN),) * (N_X - 1) + (f32(BLOCK, E),),
        in_specs=[SMEM, VMEM, VMEM, ANY, ANY, ANY],
        out_specs=(ANY, ANY, ANY, VMEM),
        input_output_aliases={3: 0, 4: 1, 5: 2},
        scratch_shapes=[pltpu.SemaphoreType.DMA((N_X - 1,))],
        compiler_params=params(8),
        cost_estimate=cost(0, 2**19),
    )(hot, mine, other, *homeward)


def hot_first_kernel(slots, hot, table, incoming, out0, out1, out2, out3):
    rep = lax.axis_index("rep")
    for ahead, out in enumerate((out0, out1, out2, out3)):
        block = lax.rem(hot[0, lax.rem(rep // 2 + ahead, N_X)], BLK_DEV)
        came = lax.fori_loop(
            0, SWAPS, lambda j, found: jnp.where(slots[0, j] == block, j, found), -1
        )

        @pl.when(came >= 0)
        def _():
            out[...] = incoming[jnp.maximum(came, 0)]

        @pl.when(came < 0)
        def _():
            out[...] = table[block]


def hot_first(slots, hot, blocks, incoming):
    return pl.pallas_call(
        hot_first_kernel,
        out_shape=(f32(BLOCK, E),) * N_X,
        in_specs=[SMEM, SMEM, VMEM, VMEM],
        out_specs=(VMEM,) * N_X,
        compiler_params=params(16),
        cost_estimate=cost(0, 2**20),
    )(slots, hot, blocks, incoming)


def hot_pick_kernel(hot, in0, in1, in2, in3, out):
    x = lax.axis_index("rep") // 2
    owner_x = hot[0, x] // (2 * BLK_DEV)
    behind = lax.rem(x - owner_x + N_X, N_X)
    for back, source in enumerate((in0, in1, in2, in3)):

        @pl.when(behind == back)
        def _():
            out[...] = source[...]


def hot_pick(hot, pieces):
    return pl.pallas_call(
        hot_pick_kernel,
        out_shape=f32(BLOCK, E),
        in_specs=[SMEM] + [VMEM] * N_X,
        out_specs=VMEM,
        compiler_params=params(8),
        cost_estimate=cost(0, 2**18),
    )(hot, *pieces)


def table_kernel(slots, table, incoming, out, came, sems):
    def clear(b, carry):
        came[b] = -1
        return carry

    def mark(j, carry):
        came[slots[0, j]] = j
        return carry

    def send(b, carry):
        @pl.when(came[b] >= 0)
        def _():
            pltpu.make_async_copy(incoming.at[jnp.maximum(came[b], 0)], out.at[b], sems.at[b]).start()

        @pl.when(came[b] < 0)
        def _():
            pltpu.make_async_copy(table.at[b], out.at[b], sems.at[b]).start()

        return carry

    def receive(b, carry):
        pltpu.make_async_copy(table.at[b], out.at[b], sems.at[b]).wait()
        return carry

    lax.fori_loop(0, BLK_DEV, clear, 0)
    lax.fori_loop(0, SWAPS, mark, 0)
    lax.fori_loop(0, BLK_DEV, send, 0)
    lax.fori_loop(0, BLK_DEV, receive, 0)


def table_after(slots, blocks, incoming):
    return pl.pallas_call(
        table_kernel,
        out_shape=f32(BLK_DEV, BLOCK, E),
        in_specs=[SMEM, VMEM, VMEM],
        out_specs=ANY,
        scratch_shapes=[pltpu.SMEM((BLK_DEV,), jnp.int32), pltpu.SemaphoreType.DMA((BLK_DEV,))],
        compiler_params=params(16),
        cost_estimate=cost(0, 2**22),
    )(slots, blocks, incoming)


def finish_kernel(counts, hot, in0, in1, in2, in3, other, pooled, hot_cache, sems):
    rep = lax.axis_index("rep")
    x = rep // 2
    blocks = (hot, in1.at[E:], in2.at[E:], in3.at[E:])
    copies = [
        pltpu.make_async_copy(block, hot_cache.at[lax.rem(x - back + N_X, N_X)], sems.at[back])
        for back, block in enumerate(blocks)
    ]
    for copy in copies:
        copy.start()
    total = in0[...] + in1[:E] + in2[:E] + in3[:E] + other[...]
    start = pl.multiple_of(rep * OWN, OWN)
    mean = total / counts[:, pl.ds(start, OWN)].astype(jnp.float32)
    pooled[...] = mean.T
    for copy in copies:
        copy.wait()


def finish(counts, hot, pieces, other):
    return pl.pallas_call(
        finish_kernel,
        out_shape=(f32(OWN, E), f32(HOT, BLOCK, E)),
        in_specs=[VMEM] * 7,
        out_specs=(VMEM, ANY),
        scratch_shapes=[pltpu.SemaphoreType.DMA((N_X,))],
        compiler_params=params(16),
        cost_estimate=cost(2**19, 2**21),
    )(counts, hot, *pieces, other)


def ahead_by(step):
    return [(x * 2 + z, (x + step) % N_X * 2 + z) for x in range(N_X) for z in range(2)]


def to_all_x(pieces):
    moved = {n: lax.ppermute(pieces[n], "rep", ahead_by(n)) for n in (2, 1, 3)}
    return [pieces[0], moved[1], moved[2], moved[3]]


def other_side(value):
    return lax.ppermute(value, "rep", [(r, r ^ 1) for r in range(N_REP)])


def body(table, swap_mask, swap_slots, hot_ids, req_idx, req_count):
    blocks = table.reshape(BLK_DEV, BLOCK, E)
    keys = req_idx[0].T
    leaving = outgoing(swap_slots, blocks)

    def branch(mask, operands):
        leaving, slots, hot, keys, counts, blocks = operands
        arrived = leaving
        if mask > 0:
            arrived = lax.ppermute(leaving, "shard", [(s, s ^ mask * 2) for s in range(N_SHARD)])
        return (arrived, *early(slots, hot, keys, counts, blocks))

    mask = swap_mask[0]
    arrived, sums, later = lax.switch(
        mask // 2,
        [functools.partial(branch, part) for part in range(N_SHARD // 2)],
        (leaving, swap_slots, hot_ids, keys, req_count, blocks),
    )
    incoming = lax.cond(
        mask % 2 == 1,
        lambda value: lax.ppermute(value, "shard", [(s, s ^ 1) for s in range(N_SHARD)]),
        lambda value: value,
        arrived,
    )
    hot_pieces = to_all_x(hot_first(swap_slots, hot_ids, blocks, incoming))
    *away, parts = late(sums, later, incoming)
    away = to_all_x(away)
    hot_mine = hot_pick(hot_ids, hot_pieces)
    own, *homeward = home(sums, later, parts)
    *homeward, hot_block = add_hot(hot_ids, hot_mine, other_side(hot_mine), homeward)
    crossing = other_side(away[0] + away[1] + away[2] + away[3])
    homeward = to_all_x([own, *homeward])
    after = table_after(swap_slots, blocks, incoming)
    pooled, hot_cache = finish(req_count, hot_block, homeward, crossing)
    return after.reshape(table.shape), hot_cache.reshape(1, HOT * BLOCK, E), pooled[None]


def solution(mesh):
    placed = (
        P(("shard", "rep"), None),
        P("rep"),
        P(("shard", "rep"), None),
        P("shard", None),
        P("shard", None, None),
        P("shard", None),
    )
    return jax.shard_map(
        body,
        mesh=mesh,
        in_specs=placed,
        out_specs=(P(("shard", "rep"), None), P("shard", None, None), P("shard", "rep", None)),
        check_vma=False,
    )
```

profile of v0, /device:TPU:32, one launch (start us, length us, event | category | flops | bytes accessed | tf_op | source)
XLA Modules:
  0.0 103.8 jit_solution(5530625087965684691)
XLA Ops:
  0.6 0.0 copy-start.4
  0.6 0.0 copy-start
  0.7 0.0 copy-start.3
  0.7 0.0 copy-start.2
  0.7 0.0 copy-start.5
  1.5 2.0 %shard_map.85 = f32[8,128,256]{2,1,0:T(8,128)S(1)} custom-call(s32[1,8]{1,0:T(1,128)} %slots.5, f32[16,128,256]{2,1,0:T(8,128)} %bitcast.12), custom_call_target="tpu_custom_call" | custom-call | bytes 2097152 | tf_op jit(solution)/shard_map/pallas_call | solution.py:62
  3.6 0.0 copy-done.4
  3.6 0.0 copy-done
  3.6 0.0 copy-done.3
  3.6 0.0 copy-done.2
  3.6 0.0 copy-done.5
  3.6 49.1 %conditional.2 = (f32[8,128,256]{2,1,0:T(8,128)S(1)}, f32[8,256,256]{2,1,0:T(8,128)}, bf16[9,1024,256]{2,1,0:T(8,128)(2,1)}) conditional(s32[]{:T(128)} %clamp.3, (s32[1,8]{1,0:T(1,128)S(1)}, s32[1,4]{1,0:T(1,128)S(1)}, s32[16,2048]{1,0:T(8,128)S(1)}, s32[1,2048]{1,0:T(1,128)S(1)}, f32[16,128,256]{2,1,0:T(8,128)S(1)}, ...), branch_computations={%region_0.1_spmd, %region_1.2_spmd, %region_2.3_spmd, %region_3.4_... | conditional | flops 17179869184 | bytes 39845952 | solution.py:399
  3.6 4.4 %collective-permute-start.5 = (f32[8,128,256]{2,1,0:T(8,128)S(1)}, f32[8,128,256]{2,1,0:T(8,128)S(1)}, u32[]{:S(2)}, u32[]{:S(2)}) collective-permute-start(f32[8,128,256]{2,1,0:T(8,128)S(1)} %get-tuple-element.245), channel_id=1, source_target_pairs={{0,96},{8,104},{16,112},{24,120},{32,64},{40,72},{48,80},{56,88},{... | collective-permute-start | bytes 3145736 | tf_op jit(solution)/shard_map/cond/branch_6_fun/ppermute | solution.py:395
  8.0 33.0 %branch_6_fun.1 = (f32[8,256,256]{2,1,0:T(8,128)}, bf16[9,1024,256]{2,1,0:T(8,128)(2,1)}) custom-call(s32[1,8]{1,0:T(1,128)S(1)} %get-tuple-element.246.slots, s32[1,4]{1,0:T(1,128)S(1)} %get-tuple-element.247.hot, s32[16,2048]{1,0:T(8,128)S(1)} %get-tuple-element.248.raw_keys, s32[1,2048]{1,0:T(1,128)S(1)} %get-tuple-element.249.counts, ...), custom_call_target="tpu_custom_call" | custom-call | flops 17179869184 | bytes 33554432 | tf_op jit(solution)/shard_map/cond/branch_6_fun/pallas_call | solution.py:159
  41.0 11.5 %collective-permute-done.5 = f32[8,128,256]{2,1,0:T(8,128)S(1)} collective-permute-done((f32[8,128,256]{2,1,0:T(8,128)S(1)}, f32[8,128,256]{2,1,0:T(8,128)S(1)}, u32[]{:S(2)}, u32[]{:S(2)}) %collective-permute-start.5) | collective-permute-done | bytes 1048608 | tf_op jit(solution)/shard_map/cond/branch_6_fun/ppermute | solution.py:395
  52.5 0.1 copy.30
  52.8 2.9 %conditional.3 = (f32[8,128,256]{2,1,0:T(8,128)S(1)}) conditional(s32[]{:T(128)} %convert_element_type.3, f32[8,128,256]{2,1,0:T(8,128)S(1)} %get-tuple-element.350, f32[8,128,256]{2,1,0:T(8,128)S(1)} %get-tuple-element.350), branch_computations={%region_16.17_spmd, %region_17.18_spmd} | conditional | bytes 6291504 | solution.py:404
  52.8 0.1 collective-permute-start.15
  52.9 2.6 %collective-permute-done.15 = f32[8,128,256]{2,1,0:T(8,128)S(1)} collective-permute-done((f32[8,128,256]{2,1,0:T(8,128)S(1)}, f32[8,128,256]{2,1,0:T(8,128)S(1)}, u32[]{:S(2)}, u32[]{:S(2)}) %collective-permute-start.15) | collective-permute-done | bytes 1048608 | tf_op jit(solution)/shard_map/cond/branch_1_fun/ppermute | solution.py:406
  55.5 0.1 copy.61
  55.6 0.0 copy-start.1
  55.6 1.0 shard_map.87
  56.6 0.1 collective-permute-start.16
  56.7 4.4 %collective-permute-start.17 = (f32[128,256]{1,0:T(8,128)S(1)}, f32[128,256]{1,0:T(8,128)S(1)}, u32[]{:S(2)}, u32[]{:S(2)}) collective-permute-start(f32[128,256]{1,0:T(8,128)S(1)} %get-tuple-element.353), channel_id=1, source_target_pairs={{0,4},{1,5},{2,6},{3,7},{4,0},{5,1},{6,2},{7,3},{8,12},{9,13},{10,... | collective-permute-start | bytes 393224 | tf_op jit(solution)/shard_map/ppermute | solution.py:378
  61.1 2.5 %collective-permute-start.18 = (f32[128,256]{1,0:T(8,128)S(1)}, f32[128,256]{1,0:T(8,128)S(1)}, u32[]{:S(2)}, u32[]{:S(2)}) collective-permute-start(f32[128,256]{1,0:T(8,128)S(1)} %get-tuple-element.354), channel_id=1, source_target_pairs={{0,6},{1,7},{2,0},{3,1},{4,2},{5,3},{6,4},{7,5},{8,14},{9,15},{10,... | collective-permute-start | bytes 393224 | tf_op jit(solution)/shard_map/ppermute | solution.py:378
  63.6 0.0 copy-done.1
  63.7 3.6 %shard_map.89 = (f32[256,256]{1,0:T(8,128)S(1)}, f32[256,256]{1,0:T(8,128)S(1)}, f32[256,256]{1,0:T(8,128)S(1)}, f32[256,256]{1,0:T(8,128)S(1)}, bf16[512,1024]{1,0:T(8,128)(2,1)S(1)}) custom-call(f32[8,256,256]{2,1,0:T(8,128)S(1)} %copy-done.1, bf16[9,1024,256]{2,1,0:T(8,128)(2,1)} %get-tuple-element.356.later, f32[8,128,256]{2,1,0:T(8,128)S(1)} %get-tuple-element.420.incoming), custom_call_target="tpu_custom_call" | custom-call | flops 1073741824 | bytes 4194304 | tf_op jit(solution)/shard_map/pallas_call | solution.py:189
  67.3 0.1 collective-permute-start.23
  67.4 1.5 %collective-permute-start.24 = (f32[256,256]{1,0:T(8,128)S(1)}, f32[256,256]{1,0:T(8,128)S(1)}, u32[]{:S(2)}, u32[]{:S(2)}) collective-permute-start(f32[256,256]{1,0:T(8,128)S(1)} %get-tuple-element.368), channel_id=1, source_target_pairs={{0,4},{1,5},{2,6},{3,7},{4,0},{5,1},{6,2},{7,3},{8,12},{9,13},{10,... | collective-permute-start | bytes 786440 | tf_op jit(solution)/shard_map/ppermute | solution.py:378
  68.8 0.0 collective-permute-done.16.in1
  68.9 1.8 %collective-permute-start.25 = (f32[256,256]{1,0:T(8,128)S(1)}, f32[256,256]{1,0:T(8,128)S(1)}, u32[]{:S(2)}, u32[]{:S(2)}) collective-permute-start(f32[256,256]{1,0:T(8,128)S(1)} %get-tuple-element.369), channel_id=1, source_target_pairs={{0,6},{1,7},{2,0},{3,1},{4,2},{5,3},{6,4},{7,5},{8,14},{9,15},{10,... | collective-permute-start | bytes 786440 | tf_op jit(solution)/shard_map/ppermute | solution.py:378
  70.6 0.0 collective-permute-done.17.in2
  70.6 0.0 collective-permute-done.18.in3
  70.6 0.6 shard_map.88.mine
  71.2 0.1 collective-permute-start.19
  71.3 3.6 %shard_map.90 = (f32[256,256]{1,0:T(8,128)S(1)}, f32[384,256]{1,0:T(8,128)S(1)}, f32[384,256]{1,0:T(8,128)S(1)}, f32[384,256]{1,0:T(8,128)S(1)}) custom-call(f32[8,256,256]{2,1,0:T(8,128)S(1)} %copy-done.1, bf16[9,1024,256]{2,1,0:T(8,128)(2,1)} %get-tuple-element.356.later, bf16[512,1024]{1,0:T(8,128)(2,1)S(1)} %get-tuple-element.357.parts), custom_call_target="tpu_custom_call" | custom-call | flops 1073741824 | bytes 4194304 | tf_op jit(solution)/shard_map/pallas_call | solution.py:206
  74.9 6.9 %collective-permute-done.19.other = f32[128,256]{1,0:T(8,128)S(1)} collective-permute-done((f32[128,256]{1,0:T(8,128)S(1)}, f32[128,256]{1,0:T(8,128)S(1)}, u32[]{:S(2)}, u32[]{:S(2)}) %collective-permute-start.19) | collective-permute-done | bytes 131104 | tf_op jit(solution)/shard_map/ppermute | solution.py:383
  81.8 1.1 %shard_map.91 = (f32[384,256]{1,0:T(8,128)S(1)}, f32[384,256]{1,0:T(8,128)S(1)}, f32[384,256]{1,0:T(8,128)S(1)}, f32[128,256]{1,0:T(8,128)S(1)}) custom-call(s32[1,4]{1,0:T(1,128)S(1)} %copy-done.3, f32[128,256]{1,0:T(8,128)S(1)} %shard_map.88.mine, ...), custom_call_target="tpu_custom_call", output_to_operand_aliasing={{0}: (3, {}), {1}: (4, {}), {2}: (5, {})} | custom-call | bytes 524288 | tf_op jit(solution)/shard_map/pallas_call | solution.py:239
  83.0 0.9 collective-permute-start.20
  83.8 1.8 %collective-permute-start.21 = (f32[384,256]{1,0:T(8,128)S(1)}, f32[384,256]{1,0:T(8,128)S(1)}, u32[]{:S(2)}, u32[]{:S(2)}) collective-permute-start(f32[384,256]{1,0:T(8,128)S(1)} %get-tuple-element.364), channel_id=1, source_target_pairs={{0,4},{1,5},{2,6},{3,7},{4,0},{5,1},{6,2},{7,3},{8,12},{9,13},{10,... | collective-permute-start | bytes 1179656 | tf_op jit(solution)/shard_map/ppermute | solution.py:378
  85.7 0.0 collective-permute-done.23
  85.7 1.9 %collective-permute-start.22 = (f32[384,256]{1,0:T(8,128)S(1)}, f32[384,256]{1,0:T(8,128)S(1)}, u32[]{:S(2)}, u32[]{:S(2)}) collective-permute-start(f32[384,256]{1,0:T(8,128)S(1)} %get-tuple-element.365), channel_id=1, source_target_pairs={{0,6},{1,7},{2,0},{3,1},{4,2},{5,3},{6,4},{7,5},{8,14},{9,15},{10,... | collective-permute-start | bytes 1179656 | tf_op jit(solution)/shard_map/ppermute | solution.py:378
  87.6 0.0 collective-permute-done.24
  87.6 0.0 collective-permute-done.25
  87.6 0.1 add_add_fusion
  87.7 0.8 collective-permute-start.26
  88.5 2.2 %shard_map.86 = f32[16,128,256]{2,1,0:T(8,128)} custom-call(s32[1,8]{1,0:T(1,128)S(1)} %copy-done.4, f32[16,128,256]{2,1,0:T(8,128)S(1)} %bitcast.30, f32[8,128,256]{2,1,0:T(8,128)S(1)} %get-tuple-element.420.incoming), custom_call_target="tpu_custom_call" | custom-call | bytes 4194304 | tf_op jit(solution)/shard_map/pallas_call | solution.py:332
  90.7 10.6 %collective-permute-done.26.other = f32[256,256]{1,0:T(8,128)S(1)} collective-permute-done((f32[256,256]{1,0:T(8,128)S(1)}, f32[256,256]{1,0:T(8,128)S(1)}, u32[]{:S(2)}, u32[]{:S(2)}) %collective-permute-start.26) | collective-permute-done | bytes 262176 | tf_op jit(solution)/shard_map/ppermute | solution.py:383
  101.2 0.0 collective-permute-done.20.in1
  101.2 0.7 collective-permute-done.21.in2
  101.9 0.2 collective-permute-done.22.in3
  102.1 1.6 %shard_map.92 = (f32[256,256]{1,0:T(8,128)}, f32[4,128,256]{2,1,0:T(8,128)}) custom-call(s32[1,2048]{1,0:T(1,128)S(1)} %copy-done.2, f32[128,256]{1,0:T(8,128)S(1)} %get-tuple-element.361.hot, f32[256,256]{1,0:T(8,128)S(1)} %get-tuple-element.362.in0, f32[384,256]{1,0:T(8,128)S(1)} %collective-permute-done.20.in1, ...), custom_call_target="tpu_custom_call" | custom-call | flops 524288 | bytes 2097152 | tf_op jit(solution)/shard_map/pallas_call | solution.py:362
Async XLA Ops:
  0.6 2.9 %copy-start.4 = (s32[1,8]{1,0:T(1,128)S(1)}, s32[1,8]{1,0:T(1,128)}, u32[]{:S(2)}) copy-start(s32[1,8]{1,0:T(1,128)} %slots.5) | copy-start | bytes 100
  0.6 2.9 %copy-start = (f32[2048,256]{1,0:T(8,128)S(1)}, f32[2048,256]{1,0:T(8,128)}, u32[]{:S(2)}) copy-start(f32[2048,256]{1,0:T(8,128)} %param.24) | copy-start | bytes 6291460
  0.7 2.9 %copy-start.3 = (s32[1,4]{1,0:T(1,128)S(1)}, s32[1,4]{1,0:T(1,128)}, u32[]{:S(2)}) copy-start(s32[1,4]{1,0:T(1,128)} %hot.5) | copy-start | bytes 52
  0.7 2.9 %copy-start.2 = (s32[1,2048]{1,0:T(1,128)S(1)}, s32[1,2048]{1,0:T(1,128)}, u32[]{:S(2)}) copy-start(s32[1,2048]{1,0:T(1,128)} %counts.1) | copy-start | bytes 24580
  0.7 2.9 %copy-start.5 = (s32[1,2048,16]{1,2,0:T(8,128)S(1)}, s32[1,2048,16]{1,2,0:T(8,128)}, u32[]{:S(2)}) copy-start(s32[1,2048,16]{1,2,0:T(8,128)} %param.28) | copy-start | bytes 393220
  3.6 48.8 %collective-permute-start.5 = (f32[8,128,256]{2,1,0:T(8,128)S(1)}, f32[8,128,256]{2,1,0:T(8,128)S(1)}, u32[]{:S(2)}, u32[]{:S(2)}) collective-permute-start(f32[8,128,256]{2,1,0:T(8,128)S(1)} %get-tuple-element.245), channel_id=1, source_target_pairs={{0,96},{8,104},{16,112},{24,120},{32,64},{40,72},{48,80},{56,88},{... | collective-permute-start | bytes 3145736 | tf_op jit(solution)/shard_map/cond/branch_6_fun/ppermute | solution.py:395
  52.8 2.7 %collective-permute-start.15 = (f32[8,128,256]{2,1,0:T(8,128)S(1)}, f32[8,128,256]{2,1,0:T(8,128)S(1)}, u32[]{:S(2)}, u32[]{:S(2)}) collective-permute-start(f32[8,128,256]{2,1,0:T(8,128)S(1)} %param.17), channel_id=1, source_target_pairs={{0,8},{8,0},{16,24},{24,16},{32,40},{40,32},{48,56},{56,48},{64,72... | collective-permute-start | bytes 3145736 | tf_op jit(solution)/shard_map/cond/branch_1_fun/ppermute | solution.py:406
  55.6 8.0 %copy-start.1 = (f32[8,256,256]{2,1,0:T(8,128)S(1)}, f32[8,256,256]{2,1,0:T(8,128)}, u32[]{:S(2)}) copy-start(f32[8,256,256]{2,1,0:T(8,128)} %get-tuple-element.355.sums) | copy-start | bytes 6291460
  56.6 12.2 %collective-permute-start.16 = (f32[128,256]{1,0:T(8,128)S(1)}, f32[128,256]{1,0:T(8,128)S(1)}, u32[]{:S(2)}, u32[]{:S(2)}) collective-permute-start(f32[128,256]{1,0:T(8,128)S(1)} %get-tuple-element.352), channel_id=1, source_target_pairs={{0,2},{1,3},{2,4},{3,5},{4,6},{5,7},{6,0},{7,1},{8,10},{9,11},{10,... | collective-permute-start | bytes 393224 | tf_op jit(solution)/shard_map/ppermute | solution.py:378
  56.7 13.9 %collective-permute-start.17 = (f32[128,256]{1,0:T(8,128)S(1)}, f32[128,256]{1,0:T(8,128)S(1)}, u32[]{:S(2)}, u32[]{:S(2)}) collective-permute-start(f32[128,256]{1,0:T(8,128)S(1)} %get-tuple-element.353), channel_id=1, source_target_pairs={{0,4},{1,5},{2,6},{3,7},{4,0},{5,1},{6,2},{7,3},{8,12},{9,13},{10,... | collective-permute-start | bytes 393224 | tf_op jit(solution)/shard_map/ppermute | solution.py:378
  61.1 9.5 %collective-permute-start.18 = (f32[128,256]{1,0:T(8,128)S(1)}, f32[128,256]{1,0:T(8,128)S(1)}, u32[]{:S(2)}, u32[]{:S(2)}) collective-permute-start(f32[128,256]{1,0:T(8,128)S(1)} %get-tuple-element.354), channel_id=1, source_target_pairs={{0,6},{1,7},{2,0},{3,1},{4,2},{5,3},{6,4},{7,5},{8,14},{9,15},{10,... | collective-permute-start | bytes 393224 | tf_op jit(solution)/shard_map/ppermute | solution.py:378
  67.3 18.4 %collective-permute-start.23 = (f32[256,256]{1,0:T(8,128)S(1)}, f32[256,256]{1,0:T(8,128)S(1)}, u32[]{:S(2)}, u32[]{:S(2)}) collective-permute-start(f32[256,256]{1,0:T(8,128)S(1)} %get-tuple-element.367), channel_id=1, source_target_pairs={{0,2},{1,3},{2,4},{3,5},{4,6},{5,7},{6,0},{7,1},{8,10},{9,11},{10,... | collective-permute-start | bytes 786440 | tf_op jit(solution)/shard_map/ppermute | solution.py:378
  67.4 20.2 %collective-permute-start.24 = (f32[256,256]{1,0:T(8,128)S(1)}, f32[256,256]{1,0:T(8,128)S(1)}, u32[]{:S(2)}, u32[]{:S(2)}) collective-permute-start(f32[256,256]{1,0:T(8,128)S(1)} %get-tuple-element.368), channel_id=1, source_target_pairs={{0,4},{1,5},{2,6},{3,7},{4,0},{5,1},{6,2},{7,3},{8,12},{9,13},{10,... | collective-permute-start | bytes 786440 | tf_op jit(solution)/shard_map/ppermute | solution.py:378
  68.9 18.8 %collective-permute-start.25 = (f32[256,256]{1,0:T(8,128)S(1)}, f32[256,256]{1,0:T(8,128)S(1)}, u32[]{:S(2)}, u32[]{:S(2)}) collective-permute-start(f32[256,256]{1,0:T(8,128)S(1)} %get-tuple-element.369), channel_id=1, source_target_pairs={{0,6},{1,7},{2,0},{3,1},{4,2},{5,3},{6,4},{7,5},{8,14},{9,15},{10,... | collective-permute-start | bytes 786440 | tf_op jit(solution)/shard_map/ppermute | solution.py:378
  71.2 10.6 %collective-permute-start.19 = (f32[128,256]{1,0:T(8,128)S(1)}, f32[128,256]{1,0:T(8,128)S(1)}, u32[]{:S(2)}, u32[]{:S(2)}) collective-permute-start(f32[128,256]{1,0:T(8,128)S(1)} %shard_map.88.mine), channel_id=1, source_target_pairs={{0,1},{1,0},{2,3},{3,2},{4,5},{5,4},{6,7},{7,6},{8,9},{9,8},{10,11... | collective-permute-start | bytes 393224 | tf_op jit(solution)/shard_map/ppermute | solution.py:383
  83.0 18.3 %collective-permute-start.20 = (f32[384,256]{1,0:T(8,128)S(1)}, f32[384,256]{1,0:T(8,128)S(1)}, u32[]{:S(2)}, u32[]{:S(2)}) collective-permute-start(f32[384,256]{1,0:T(8,128)S(1)} %get-tuple-element.363), channel_id=1, source_target_pairs={{0,2},{1,3},{2,4},{3,5},{4,6},{5,7},{6,0},{7,1},{8,10},{9,11},{10,... | collective-permute-start | bytes 1179656 | tf_op jit(solution)/shard_map/ppermute | solution.py:378
  83.8 18.1 %collective-permute-start.21 = (f32[384,256]{1,0:T(8,128)S(1)}, f32[384,256]{1,0:T(8,128)S(1)}, u32[]{:S(2)}, u32[]{:S(2)}) collective-permute-start(f32[384,256]{1,0:T(8,128)S(1)} %get-tuple-element.364), channel_id=1, source_target_pairs={{0,4},{1,5},{2,6},{3,7},{4,0},{5,1},{6,2},{7,3},{8,12},{9,13},{10,... | collective-permute-start | bytes 1179656 | tf_op jit(solution)/shard_map/ppermute | solution.py:378
  85.7 16.4 %collective-permute-start.22 = (f32[384,256]{1,0:T(8,128)S(1)}, f32[384,256]{1,0:T(8,128)S(1)}, u32[]{:S(2)}, u32[]{:S(2)}) collective-permute-start(f32[384,256]{1,0:T(8,128)S(1)} %get-tuple-element.365), channel_id=1, source_target_pairs={{0,6},{1,7},{2,0},{3,1},{4,2},{5,3},{6,4},{7,5},{8,14},{9,15},{10,... | collective-permute-start | bytes 1179656 | tf_op jit(solution)/shard_map/ppermute | solution.py:378
  87.7 13.5 %collective-permute-start.26 = (f32[256,256]{1,0:T(8,128)S(1)}, f32[256,256]{1,0:T(8,128)S(1)}, u32[]{:S(2)}, u32[]{:S(2)}) collective-permute-start(f32[256,256]{1,0:T(8,128)S(1)} %add_add_fusion), channel_id=1, source_target_pairs={{0,1},{1,0},{2,3},{3,2},{4,5},{5,4},{6,7},{7,6},{8,9},{9,8},{10,11... | collective-permute-start | bytes 786440 | tf_op jit(solution)/shard_map/ppermute | solution.py:383
where the time goes:
time: 105 us; the launch traced here: 104 us
  Pallas kernels  48.7 us (46%)
  waiting for transfers between devices  32.5 us (31%)
  starting transfers between devices  20.3 us (19%)
  between operations  1.84 us (2%)
    pallas_call x1, Pallas kernels, early(): pl.pallas_call(early_kernel, out_shape=(f32(PIECES, E, OWN), jax.ShapeDty...  33 us
    ppermute x2, waiting for transfers between devices, other_side(): return lax.ppermute(value, 'rep', [(r, r ^ 1) for r in range(N_REP)])  17.5 us
    ppermute x9, starting transfers between devices, to_all_x(): moved = {n: lax.ppermute(pieces[n], 'rep', ahead_by(n)) for n in (2, 1, 3)}  15 us
    ppermute x1, waiting for transfers between devices, branch(): lax.ppermute(leaving, 'shard', [(s, s ^ mask * 2) for s in range(N_SHARD)])  11.5 us
    ppermute x1, starting transfers between devices, branch(): lax.ppermute(leaving, 'shard', [(s, s ^ mask * 2) for s in range(N_SHARD)])  4.37 us
    pallas_call x1, Pallas kernels, late(): pl.pallas_call(late_kernel, out_shape=(f32(E, OWN),) * N_X + (jax.ShapeDt...  3.64 us
    pallas_call x1, Pallas kernels, home(): pl.pallas_call(home_kernel, out_shape=(f32(E, OWN),) + (f32(E + BLOCK, OW...  3.58 us
    ppermute x1, waiting for transfers between devices, body(): lax.ppermute(value, 'shard', [(s, s ^ 1) for s in range(N_SHARD)])  2.64 us
  transfers between devices with their start and end apart: 13, of which 6 were waited for; matrix products, arithmetic and copies ran while one was open for 0% of the time, Pallas kernels for 42%

commit v1 on v0

--- a/solution.py
+++ b/solution.py
@@ -29,6 +29,10 @@
 ANY = pl.BlockSpec(memory_space=pl.ANY)
 
 
+def in_vmem(value):
+    return pltpu.with_memory_space_constraint(value, pltpu.VMEM)
+
+
 def f32(*shape):
     return jax.ShapeDtypeStruct(shape, jnp.float32)
 
@@ -69,7 +73,7 @@
     )(slots, blocks)
 
 
-def early_kernel(slots, hot, raw_keys, counts, table, sums, later, keys, flags, order, parts):
+def early_kernel(slots, hot, raw_keys, counts, table, sums, later_away, later_home, hot_kept, keys, flags, order, parts, now):
     rep = lax.axis_index("rep")
 
     def clear(b, carry):
@@ -99,6 +103,11 @@
         return carry
 
     lax.fori_loop(0, SWAPS, split, 0)
+    def keep_hot(n, carry):
+        hot_kept[n] = table[lax.rem(hot[0, lax.rem(rep // 2 + n + 1, N_X)], BLK_DEV)]
+        return carry
+
+    lax.fori_loop(0, N_X - 1, keep_hot, 0)
     row_in_tile = lax.broadcasted_iota(jnp.int32, (16, 128), 0).astype(COUNT_INT)
     one, zero = jnp.bfloat16(1), jnp.bfloat16(0)
 
@@ -110,23 +119,40 @@
             side = step % 2 * 128
             lanes = pl.multiple_of(start + side, 128)
             column = pl.multiple_of(side, 128)
-            place = jnp.where(j < SWAPS, PIECES, piece)
             first = (rep * BLK_DEV + order[j]) * BLOCK
             near = []
             for k in range(K):
                 offset = jnp.clip(keys[pl.ds(k, 1), pl.ds(lanes, 128)] - first, -1, BLOCK)
                 near.append(jnp.broadcast_to(offset, (16, 128)).astype(COUNT_INT))
+            tiles = []
             for tile in range(BLOCK // 16):
                 row = row_in_tile + jnp.array(tile * 16, COUNT_INT)
                 total = jnp.where(near[0] == row, one, zero)
                 for k in range(1, K):
                     total = total + jnp.where(near[k] == row, one, zero)
-                row0 = pl.multiple_of(j % SWAPS * BLOCK + tile * 16, 16)
-                later[place, pl.ds(row0, 16), pl.ds(column, 128)] = total
+                tiles.append(total)
+            row0 = pl.multiple_of(j % SWAPS * BLOCK, BLOCK)
+
+            def keep(place):
+                for tile, total in enumerate(tiles):
+                    place[pl.ds(row0 + tile * 16, 16), pl.ds(column, 128)] = total
+
+            @pl.when(j < SWAPS)
+            def _():
+                keep(now)
+
+            @pl.when(jnp.logical_and(j >= SWAPS, piece < N_X))
+            def _():
+                keep(later_away.at[jnp.minimum(piece, N_X - 1)])
+
+            @pl.when(jnp.logical_and(j >= SWAPS, piece >= N_X))
+            def _():
+                keep(later_home.at[jnp.maximum(piece - N_X, 0)])
+
             return inner
 
         lax.fori_loop(0, BLK_DEV * 2, one_block, 0)
-        apply_counts(parts, later.at[PIECES], sums.at[piece])
+        apply_counts(parts, now, sums.at[piece])
         return carry
 
     lax.fori_loop(0, PIECES, one_piece, 0)
@@ -160,54 +186,65 @@
         early_kernel,
         out_shape=(
             f32(PIECES, E, OWN),
-            jax.ShapeDtypeStruct((PIECES + 1, HALF_ROWS, OWN), jnp.bfloat16),
+            jax.ShapeDtypeStruct((N_X, HALF_ROWS, OWN), jnp.bfloat16),
+            jax.ShapeDtypeStruct((N_X, HALF_ROWS, OWN), jnp.bfloat16),
+            f32(N_X - 1, BLOCK, E),
         ),
         in_specs=[SMEM, SMEM, VMEM, VMEM, VMEM],
-        out_specs=(VMEM, VMEM),
+        out_specs=(VMEM,) * 4,
         scratch_shapes=[
             pltpu.VMEM((K, REQS), jnp.int32),
             pltpu.SMEM((BLK_DEV,), jnp.int32),
             pltpu.SMEM((BLK_DEV,), jnp.int32),
             pltpu.VMEM((CHUNKS, 2 * WIDE, HALF_ROWS), jnp.bfloat16),
+            pltpu.VMEM((HALF_ROWS, OWN), jnp.bfloat16),
         ],
         compiler_params=params(16),
         cost_estimate=cost(2**34, 2**25),
     )(slots, hot, keys, counts, blocks)
 
 
-def late_kernel(sums, later, incoming, out0, out1, out2, out3, parts):
+def late_kernel(sums, later, incoming, out0, out1, out2, out3, parts, sums_in, sem):
+    copy = pltpu.make_async_copy(sums.at[pl.ds(0, N_X)], sums_in, sem.at[0])
+    copy.start()
     for j in range(SWAPS):
         high, low = turn_rows(incoming[j])
         parts[:E, j * BLOCK : (j + 1) * BLOCK] = high
         parts[E:, j * BLOCK : (j + 1) * BLOCK] = low
+    copy.wait()
     for ahead, out in ((2, out2), (1, out1), (3, out3), (0, out0)):
         both = jnp.dot(parts[...], later[ahead], preferred_element_type=jnp.float32)
-        out[...] = sums[ahead] + both[:E] + both[E:]
+        out[...] = sums_in[ahead] + both[:E] + both[E:]
 
 
 def late(sums, later, incoming):
     return pl.pallas_call(
         late_kernel,
         out_shape=(f32(E, OWN),) * N_X + (jax.ShapeDtypeStruct((2 * E, HALF_ROWS), jnp.bfloat16),),
-        in_specs=[VMEM] * 3,
+        in_specs=[ANY, VMEM, VMEM],
         out_specs=(VMEM,) * (N_X + 1),
+        scratch_shapes=[pltpu.VMEM((N_X, E, OWN), jnp.float32), pltpu.SemaphoreType.DMA((1,))],
         compiler_params=params(16),
         cost_estimate=cost(2**30, 2**22),
-    )(sums, later, incoming)
-
-
-def home_kernel(sums, later, parts, out0, out1, out2, out3):
+    )(sums, in_vmem(later), in_vmem(incoming))
+
+
+def home_kernel(sums, later, parts, out0, out1, out2, out3, sums_in, sem):
+    copy = pltpu.make_async_copy(sums.at[pl.ds(N_X, N_X)], sums_in, sem.at[0])
+    copy.start()
+    copy.wait()
     for ahead, out in ((2, out2), (1, out1), (3, out3), (0, out0)):
-        both = jnp.dot(parts[...], later[N_X + ahead], preferred_element_type=jnp.float32)
-        out[:E] = sums[N_X + ahead] + both[:E] + both[E:]
+        both = jnp.dot(parts[...], later[ahead], preferred_element_type=jnp.float32)
+        out[:E] = sums_in[ahead] + both[:E] + both[E:]
 
 
 def home(sums, later, parts):
     return pl.pallas_call(
         home_kernel,
         out_shape=(f32(E, OWN),) + (f32(E + BLOCK, OWN),) * (N_X - 1),
-        in_specs=[VMEM] * 3,
+        in_specs=[ANY, VMEM, VMEM],
         out_specs=(VMEM,) * N_X,
+        scratch_shapes=[pltpu.VMEM((N_X, E, OWN), jnp.float32), pltpu.SemaphoreType.DMA((1,))],
         compiler_params=params(16),
         cost_estimate=cost(2**30, 2**22),
     )(sums, later, parts)
@@ -248,13 +285,17 @@
     )(hot, mine, other, *homeward)
 
 
-def hot_first_kernel(slots, hot, table, incoming, out0, out1, out2, out3):
-    rep = lax.axis_index("rep")
-    for ahead, out in enumerate((out0, out1, out2, out3)):
-        block = lax.rem(hot[0, lax.rem(rep // 2 + ahead, N_X)], BLK_DEV)
-        came = lax.fori_loop(
-            0, SWAPS, lambda j, found: jnp.where(slots[0, j] == block, j, found), -1
-        )
+def came_from(slots, block):
+    return lax.fori_loop(
+        0, SWAPS, lambda j, found: jnp.where(slots[0, j] == block, j, found), -1
+    )
+
+
+def hot_first_kernel(slots, hot, kept, incoming, out1, out2, out3):
+    x = lax.axis_index("rep") // 2
+    for n, out in enumerate((out1, out2, out3)):
+        block = lax.rem(hot[0, lax.rem(x + n + 1, N_X)], BLK_DEV)
+        came = came_from(slots, block)
 
         @pl.when(came >= 0)
         def _():
@@ -262,40 +303,53 @@
 
         @pl.when(came < 0)
         def _():
-            out[...] = table[block]
-
-
-def hot_first(slots, hot, blocks, incoming):
+            out[...] = kept[n]
+
+
+def hot_first(slots, hot, kept, incoming):
     return pl.pallas_call(
         hot_first_kernel,
-        out_shape=(f32(BLOCK, E),) * N_X,
+        out_shape=(f32(BLOCK, E),) * (N_X - 1),
         in_specs=[SMEM, SMEM, VMEM, VMEM],
-        out_specs=(VMEM,) * N_X,
-        compiler_params=params(16),
+        out_specs=(VMEM,) * (N_X - 1),
+        compiler_params=params(8),
         cost_estimate=cost(0, 2**20),
-    )(slots, hot, blocks, incoming)
-
-
-def hot_pick_kernel(hot, in0, in1, in2, in3, out):
+    )(slots, hot, in_vmem(kept), in_vmem(incoming))
+
+
+def hot_pick_kernel(slots, hot, table, incoming, in1, in2, in3, out, sem):
     x = lax.axis_index("rep") // 2
     owner_x = hot[0, x] // (2 * BLK_DEV)
     behind = lax.rem(x - owner_x + N_X, N_X)
-    for back, source in enumerate((in0, in1, in2, in3)):
-
-        @pl.when(behind == back)
+    block = lax.rem(hot[0, x], BLK_DEV)
+    came = came_from(slots, block)
+    for n, source in enumerate((in1, in2, in3)):
+
+        @pl.when(behind == n + 1)
         def _():
             out[...] = source[...]
 
-
-def hot_pick(hot, pieces):
+    @pl.when(jnp.logical_and(behind == 0, came >= 0))
+    def _():
+        out[...] = incoming[jnp.maximum(came, 0)]
+
+    @pl.when(jnp.logical_and(behind == 0, came < 0))
+    def _():
+        copy = pltpu.make_async_copy(table.at[block], out, sem.at[0])
+        copy.start()
+        copy.wait()
+
+
+def hot_pick(slots, hot, blocks, incoming, pieces):
     return pl.pallas_call(
         hot_pick_kernel,
         out_shape=f32(BLOCK, E),
-        in_specs=[SMEM] + [VMEM] * N_X,
+        in_specs=[SMEM, SMEM, ANY, VMEM] + [VMEM] * (N_X - 1),
         out_specs=VMEM,
+        scratch_shapes=[pltpu.SemaphoreType.DMA((1,))],
         compiler_params=params(8),
         cost_estimate=cost(0, 2**18),
-    )(hot, *pieces)
+    )(slots, hot, blocks, in_vmem(incoming), *pieces)
 
 
 def table_kernel(slots, table, incoming, out, came, sems):
@@ -396,7 +450,7 @@
         return (arrived, *early(slots, hot, keys, counts, blocks))
 
     mask = swap_mask[0]
-    arrived, sums, later = lax.switch(
+    arrived, sums, later_away, later_home, hot_kept = lax.switch(
         mask // 2,
         [functools.partial(branch, part) for part in range(N_SHARD // 2)],
         (leaving, swap_slots, hot_ids, keys, req_count, blocks),
@@ -407,11 +461,11 @@
         lambda value: value,
         arrived,
     )
-    hot_pieces = to_all_x(hot_first(swap_slots, hot_ids, blocks, incoming))
-    *away, parts = late(sums, later, incoming)
+    hot_pieces = to_all_x([None, *hot_first(swap_slots, hot_ids, hot_kept, incoming)])[1:]
+    *away, parts = late(sums, later_away, incoming)
     away = to_all_x(away)
-    hot_mine = hot_pick(hot_ids, hot_pieces)
-    own, *homeward = home(sums, later, parts)
+    hot_mine = hot_pick(swap_slots, hot_ids, blocks, incoming, hot_pieces)
+    own, *homeward = home(sums, later_home, parts)
     *homeward, hot_block = add_hot(hot_ids, hot_mine, other_side(hot_mine), homeward)
     crossing = other_side(away[0] + away[1] + away[2] + away[3])
     homeward = to_all_x([own, *homeward])

time: 105 us -> 105 us (level)
  waiting for transfers between devices: 32.5 us -> 27.7 us
  Pallas kernels: 48.7 us -> 51.7 us
  starting transfers between devices: 20.3 us -> 22.9 us
    pallas_call x1, Pallas kernels: 33 us -> 39.3 us  [early(): pl.pallas_call(early_kernel, out_shape=(f32(PIECES, E, OWN), jax.ShapeDty...]
    ppermute x1, waiting for transfers between devices: 11.5 us -> 6.35 us  [branch(): lax.ppermute(leaving, 'shard', [(s, s ^ mask * 2) for s in range(N_SHARD)])]
    ppermute x2, starting transfers between devices: 0.9 us -> 5.04 us  [other_side(): return lax.ppermute(value, 'rep', [(r, r ^ 1) for r in range(N_REP)])]
    pallas_call x1, Pallas kernels: 3.58 us -> 1.33 us  [home(): pl.pallas_call(home_kernel, out_shape=(f32(E, OWN),) + (f32(E + BLOCK, OW...]
    ppermute x9, starting transfers between devices: 15 us -> 13.2 us  [to_all_x(): moved = {n: lax.ppermute(pieces[n], 'rep', ahead_by(n)) for n in (2, 1, 3)}]
    ppermute x9, waiting for transfers between devices: 0.88 us -> 2.1 us  [to_all_x(): moved = {n: lax.ppermute(pieces[n], 'rep', ahead_by(n)) for n in (2, 1, 3)}]
  transfers between devices with their start and end apart: 13 -> 13, of which waited for: 6 -> 5; matrix products, arithmetic and copies ran while one was open for 0% -> 0% of each run, Pallas kernels for 42% -> 45%
where the time goes in v1:
time: 105 us
  Pallas kernels  51.7 us (49%)
  waiting for transfers between devices  27.7 us (26%)
  starting transfers between devices  22.9 us (22%)
  between operations  1.67 us (2%)
    pallas_call x1, Pallas kernels, early(): pl.pallas_call(early_kernel, out_shape=(f32(PIECES, E, OWN), jax.ShapeDty...  39.3 us
    ppermute x2, waiting for transfers between devices, other_side(): return lax.ppermute(value, 'rep', [(r, r ^ 1) for r in range(N_REP)])  16.6 us
    ppermute x9, starting transfers between devices, to_all_x(): moved = {n: lax.ppermute(pieces[n], 'rep', ahead_by(n)) for n in (2, 1, 3)}  13.2 us
    ppermute x1, waiting for transfers between devices, branch(): lax.ppermute(leaving, 'shard', [(s, s ^ mask * 2) for s in range(N_SHARD)])  6.35 us
    ppermute x2, starting transfers between devices, other_side(): return lax.ppermute(value, 'rep', [(r, r ^ 1) for r in range(N_REP)])  5.04 us
    ppermute x1, starting transfers between devices, branch(): lax.ppermute(leaving, 'shard', [(s, s ^ mask * 2) for s in range(N_SHARD)])  4.63 us
    ppermute x1, waiting for transfers between devices, body(): lax.ppermute(value, 'shard', [(s, s ^ 1) for s in range(N_SHARD)])  2.65 us
    pallas_call x1, Pallas kernels, late(): pl.pallas_call(late_kernel, out_shape=(f32(E, OWN),) * N_X + (jax.ShapeDt...  2.63 us
  transfers between devices with their start and end apart: 13, of which 5 were waited for; matrix products, arithmetic and copies ran while one was open for 0% of the time, Pallas kernels for 45%

profile of v1, /device:TPU:32, one launch (start us, length us, event | category | flops | bytes accessed | tf_op | source)
XLA Modules:
  0.0 104.5 jit_solution(10479011492007031368)
XLA Ops:
  0.6 0.0 copy-start.4
  0.6 0.0 copy-start.5
  0.7 0.0 copy-start.3
  1.3 2.0 %shard_map.85 = f32[8,128,256]{2,1,0:T(8,128)S(1)} custom-call(s32[1,8]{1,0:T(1,128)} %slots.7, f32[16,128,256]{2,1,0:T(8,128)} %bitcast.12), custom_call_target="tpu_custom_call" | custom-call | bytes 2097152 | tf_op jit(solution)/shard_map/pallas_call | solution.py:66
  3.4 0.0 copy-done.4
  3.4 0.0 copy-done.5
  3.4 0.0 copy-done.3
  3.4 50.6 %conditional.2 = (f32[8,128,256]{2,1,0:T(8,128)S(1)}, f32[8,256,256]{2,1,0:T(8,128)}, bf16[4,1024,256]{2,1,0:T(8,128)(2,1)S(1)}, bf16[4,1024,256]{2,1,0:T(8,128)(2,1)}, f32[3,128,256]{2,1,0:T(8,128)S(1)}) conditional(s32[]{:T(128)} %clamp.3, (s32[1,8]{1,0:T(1,128)S(1)}, s32[1,4]{1,0:T(1,128)S(1)}, ...), branch_computations={%region_0.1_spmd, %region_1.2_spmd, %region_2.3_spmd, %region_3.4_... | conditional | flops 17179869184 | bytes 39845968 | solution.py:453
  3.5 4.6 %collective-permute-start.10 = (f32[8,128,256]{2,1,0:T(8,128)S(1)}, f32[8,128,256]{2,1,0:T(8,128)S(1)}, u32[]{:S(2)}, u32[]{:S(2)}) collective-permute-start(f32[8,128,256]{2,1,0:T(8,128)S(1)} %get-tuple-element.307), channel_id=1, source_target_pairs={{0,176},{8,184},{16,160},{24,168},{32,144},{40,152},{48,128},{56,1... | collective-permute-start | bytes 3145736 | tf_op jit(solution)/shard_map/cond/branch_11_fun/ppermute | solution.py:449
  8.1 39.3 %branch_11_fun.1 = (f32[8,256,256]{2,1,0:T(8,128)}, bf16[4,1024,256]{2,1,0:T(8,128)(2,1)S(1)}, bf16[4,1024,256]{2,1,0:T(8,128)(2,1)}, f32[3,128,256]{2,1,0:T(8,128)S(1)}) custom-call(s32[1,8]{1,0:T(1,128)S(1)} %get-tuple-element.308.slots, s32[1,4]{1,0:T(1,128)S(1)} %get-tuple-element.309.hot, s32[16,2048]{1,0:T(8,128)} %get-tuple-element.310.raw_keys, ...), custom_call_target="tpu_custom_call" | custom-call | flops 17179869184 | bytes 33554432 | tf_op jit(solution)/shard_map/cond/branch_11_fun/pallas_call | solution.py:185
  47.4 6.3 %collective-permute-done.10 = f32[8,128,256]{2,1,0:T(8,128)S(1)} collective-permute-done((f32[8,128,256]{2,1,0:T(8,128)S(1)}, f32[8,128,256]{2,1,0:T(8,128)S(1)}, u32[]{:S(2)}, u32[]{:S(2)}) %collective-permute-start.10) | collective-permute-done | bytes 1048608 | tf_op jit(solution)/shard_map/cond/branch_11_fun/ppermute | solution.py:449
  53.8 0.1 copy.67
  54.0 2.8 %conditional.3 = (f32[8,128,256]{2,1,0:T(8,128)S(1)}) conditional(s32[]{:T(128)} %convert_element_type.3, f32[8,128,256]{2,1,0:T(8,128)S(1)} %get-tuple-element.383, f32[8,128,256]{2,1,0:T(8,128)S(1)} %get-tuple-element.383), branch_computations={%region_16.17_spmd, %region_17.18_spmd} | conditional | bytes 6291504 | solution.py:458
  54.0 0.1 collective-permute-start.15
  54.1 2.6 %collective-permute-done.15 = f32[8,128,256]{2,1,0:T(8,128)S(1)} collective-permute-done((f32[8,128,256]{2,1,0:T(8,128)S(1)}, f32[8,128,256]{2,1,0:T(8,128)S(1)}, u32[]{:S(2)}, u32[]{:S(2)}) %collective-permute-start.15) | collective-permute-done | bytes 1048608 | tf_op jit(solution)/shard_map/cond/branch_1_fun/ppermute | solution.py:460
  56.8 0.1 copy.93
  56.9 0.9 shard_map.87
  57.7 1.4 %collective-permute-start.16 = (f32[128,256]{1,0:T(8,128)S(1)}, f32[128,256]{1,0:T(8,128)S(1)}, u32[]{:S(2)}, u32[]{:S(2)}) collective-permute-start(f32[128,256]{1,0:T(8,128)S(1)} %get-tuple-element.385), channel_id=1, source_target_pairs={{0,2},{1,3},{2,4},{3,5},{4,6},{5,7},{6,0},{7,1},{8,10},{9,11},{10,... | collective-permute-start | bytes 393224 | tf_op jit(solution)/shard_map/ppermute | solution.py:432
  59.1 0.3 collective-permute-start.17
  59.4 2.5 %collective-permute-start.18 = (f32[128,256]{1,0:T(8,128)S(1)}, f32[128,256]{1,0:T(8,128)S(1)}, u32[]{:S(2)}, u32[]{:S(2)}) collective-permute-start(f32[128,256]{1,0:T(8,128)S(1)} %get-tuple-element.387), channel_id=1, source_target_pairs={{0,6},{1,7},{2,0},{3,1},{4,2},{5,3},{6,4},{7,5},{8,14},{9,15},{10,... | collective-permute-start | bytes 393224 | tf_op jit(solution)/shard_map/ppermute | solution.py:432
  61.9 0.0 copy-start
  61.9 0.0 copy-start.2
  61.9 2.6 %shard_map.89 = (f32[256,256]{1,0:T(8,128)S(1)}, f32[256,256]{1,0:T(8,128)S(1)}, f32[256,256]{1,0:T(8,128)S(1)}, f32[256,256]{1,0:T(8,128)S(1)}, bf16[512,1024]{1,0:T(8,128)(2,1)S(1)}) custom-call(f32[8,256,256]{2,1,0:T(8,128)} %get-tuple-element.388.sums, bf16[4,1024,256]{2,1,0:T(8,128)(2,1)S(1)} %get-tuple-element.390.later, ...), custom_call_target="tpu_custom_call" | custom-call | flops 1073741824 | bytes 4194304 | tf_op jit(solution)/shard_map/pallas_call | solution.py:221
  64.5 0.0 copy-start.1
  64.6 0.1 collective-permute-start.23
  64.7 2.8 %collective-permute-start.24 = (f32[256,256]{1,0:T(8,128)S(1)}, f32[256,256]{1,0:T(8,128)S(1)}, u32[]{:S(2)}, u32[]{:S(2)}) collective-permute-start(f32[256,256]{1,0:T(8,128)S(1)} %get-tuple-element.402), channel_id=1, source_target_pairs={{0,4},{1,5},{2,6},{3,7},{4,0},{5,1},{6,2},{7,3},{8,12},{9,13},{10,... | collective-permute-start | bytes 786440 | tf_op jit(solution)/shard_map/ppermute | solution.py:432
  67.4 0.0 collective-permute-done.16.in1
  67.4 1.9 %collective-permute-start.25 = (f32[256,256]{1,0:T(8,128)S(1)}, f32[256,256]{1,0:T(8,128)S(1)}, u32[]{:S(2)}, u32[]{:S(2)}) collective-permute-start(f32[256,256]{1,0:T(8,128)S(1)} %get-tuple-element.403), channel_id=1, source_target_pairs={{0,6},{1,7},{2,0},{3,1},{4,2},{5,3},{6,4},{7,5},{8,14},{9,15},{10,... | collective-permute-start | bytes 786440 | tf_op jit(solution)/shard_map/ppermute | solution.py:432
  69.4 0.0 collective-permute-done.17.in2
  69.4 0.0 collective-permute-done.18.in3
  69.4 0.0 copy-done
  69.4 0.7 shard_map.88.mine
  70.1 2.8 %collective-permute-start.19 = (f32[128,256]{1,0:T(8,128)S(1)}, f32[128,256]{1,0:T(8,128)S(1)}, u32[]{:S(2)}, u32[]{:S(2)}) collective-permute-start(f32[128,256]{1,0:T(8,128)S(1)} %shard_map.88.mine), channel_id=1, source_target_pairs={{0,1},{1,0},{2,3},{3,2},{4,5},{5,4},{6,7},{7,6},{8,9},{9,8},{10,11... | collective-permute-start | bytes 393224 | tf_op jit(solution)/shard_map/ppermute | solution.py:437
  72.9 0.0 copy-done.2
  72.9 0.0 copy-done.1
  72.9 1.3 %shard_map.90 = (f32[256,256]{1,0:T(8,128)S(1)}, f32[384,256]{1,0:T(8,128)S(1)}, f32[384,256]{1,0:T(8,128)S(1)}, f32[384,256]{1,0:T(8,128)S(1)}) custom-call(f32[8,256,256]{2,1,0:T(8,128)S(1)} %copy-done.1, bf16[4,1024,256]{2,1,0:T(8,128)(2,1)S(1)} %copy-done.2, bf16[512,1024]{1,0:T(8,128)(2,1)S(1)} %get-tuple-element.391.parts), custom_call_target="tpu_custom_call" | custom-call | flops 1073741824 | bytes 4194304 | tf_op jit(solution)/shard_map/pallas_call | solution.py:242
  74.2 6.5 %collective-permute-done.19.other = f32[128,256]{1,0:T(8,128)S(1)} collective-permute-done((f32[128,256]{1,0:T(8,128)S(1)}, f32[128,256]{1,0:T(8,128)S(1)}, u32[]{:S(2)}, u32[]{:S(2)}) %collective-permute-start.19) | collective-permute-done | bytes 131104 | tf_op jit(solution)/shard_map/ppermute | solution.py:437
  80.7 1.1 %shard_map.91 = (f32[384,256]{1,0:T(8,128)S(1)}, f32[384,256]{1,0:T(8,128)S(1)}, f32[384,256]{1,0:T(8,128)S(1)}, f32[128,256]{1,0:T(8,128)S(1)}) custom-call(s32[1,4]{1,0:T(1,128)S(1)} %copy-done.5, f32[128,256]{1,0:T(8,128)S(1)} %shard_map.88.mine, ...), custom_call_target="tpu_custom_call", output_to_operand_aliasing={{0}: (3, {}), {1}: (4, {}), {2}: (5, {})} | custom-call | bytes 524288 | tf_op jit(solution)/shard_map/pallas_call | solution.py:276
  81.8 0.1 collective-permute-start.20
  81.9 3.5 %collective-permute-start.21 = (f32[384,256]{1,0:T(8,128)S(1)}, f32[384,256]{1,0:T(8,128)S(1)}, u32[]{:S(2)}, u32[]{:S(2)}) collective-permute-start(f32[384,256]{1,0:T(8,128)S(1)} %get-tuple-element.398), channel_id=1, source_target_pairs={{0,4},{1,5},{2,6},{3,7},{4,0},{5,1},{6,2},{7,3},{8,12},{9,13},{10,... | collective-permute-start | bytes 1179656 | tf_op jit(solution)/shard_map/ppermute | solution.py:432
  85.4 0.0 collective-permute-done.23
  85.4 0.6 collective-permute-start.22
  86.0 0.0 collective-permute-done.24
  86.0 0.0 collective-permute-done.25
  86.0 0.1 add_add_fusion
  86.1 2.3 %collective-permute-start.26 = (f32[256,256]{1,0:T(8,128)S(1)}, f32[256,256]{1,0:T(8,128)S(1)}, u32[]{:S(2)}, u32[]{:S(2)}) collective-permute-start(f32[256,256]{1,0:T(8,128)S(1)} %add_add_fusion), channel_id=1, source_target_pairs={{0,1},{1,0},{2,3},{3,2},{4,5},{5,4},{6,7},{7,6},{8,9},{9,8},{10,11... | collective-permute-start | bytes 786440 | tf_op jit(solution)/shard_map/ppermute | solution.py:437
  88.4 2.2 %shard_map.86 = f32[16,128,256]{2,1,0:T(8,128)} custom-call(s32[1,8]{1,0:T(1,128)S(1)} %copy-done.4, f32[16,128,256]{2,1,0:T(8,128)S(1)} %bitcast.30, f32[8,128,256]{2,1,0:T(8,128)S(1)} %get-tuple-element.486.incoming), custom_call_target="tpu_custom_call" | custom-call | bytes 4194304 | tf_op jit(solution)/shard_map/pallas_call | solution.py:386
  90.5 10.2 %collective-permute-done.26.other = f32[256,256]{1,0:T(8,128)S(1)} collective-permute-done((f32[256,256]{1,0:T(8,128)S(1)}, f32[256,256]{1,0:T(8,128)S(1)}, u32[]{:S(2)}, u32[]{:S(2)}) %collective-permute-start.26) | collective-permute-done | bytes 262176 | tf_op jit(solution)/shard_map/ppermute | solution.py:437
  100.7 0.0 collective-permute-done.20.in1
  100.7 2.1 %collective-permute-done.21.in2 = f32[384,256]{1,0:T(8,128)S(1)} collective-permute-done((f32[384,256]{1,0:T(8,128)S(1)}, f32[384,256]{1,0:T(8,128)S(1)}, u32[]{:S(2)}, u32[]{:S(2)}) %collective-permute-start.21) | collective-permute-done | bytes 393248 | tf_op jit(solution)/shard_map/ppermute | solution.py:432
  102.8 0.0 collective-permute-done.22.in3
  102.8 1.6 %shard_map.92 = (f32[256,256]{1,0:T(8,128)}, f32[4,128,256]{2,1,0:T(8,128)}) custom-call(s32[1,2048]{1,0:T(1,128)S(1)} %copy-done.3, f32[128,256]{1,0:T(8,128)S(1)} %get-tuple-element.395.hot, f32[256,256]{1,0:T(8,128)S(1)} %get-tuple-element.396.in0, f32[384,256]{1,0:T(8,128)S(1)} %collective-permute-done.20.in1, ...), custom_call_target="tpu_custom_call" | custom-call | flops 524288 | bytes 2097152 | tf_op jit(solution)/shard_map/pallas_call | solution.py:416
Async XLA Ops:
  0.6 2.8 %copy-start.4 = (s32[1,8]{1,0:T(1,128)S(1)}, s32[1,8]{1,0:T(1,128)}, u32[]{:S(2)}) copy-start(s32[1,8]{1,0:T(1,128)} %slots.7) | copy-start | bytes 100
  0.6 2.8 %copy-start.5 = (s32[1,4]{1,0:T(1,128)S(1)}, s32[1,4]{1,0:T(1,128)}, u32[]{:S(2)}) copy-start(s32[1,4]{1,0:T(1,128)} %hot.5) | copy-start | bytes 52
  0.7 2.8 %copy-start.3 = (s32[1,2048]{1,0:T(1,128)S(1)}, s32[1,2048]{1,0:T(1,128)}, u32[]{:S(2)}) copy-start(s32[1,2048]{1,0:T(1,128)} %counts.1) | copy-start | bytes 24580
  3.5 50.3 %collective-permute-start.10 = (f32[8,128,256]{2,1,0:T(8,128)S(1)}, f32[8,128,256]{2,1,0:T(8,128)S(1)}, u32[]{:S(2)}, u32[]{:S(2)}) collective-permute-start(f32[8,128,256]{2,1,0:T(8,128)S(1)} %get-tuple-element.307), channel_id=1, source_target_pairs={{0,176},{8,184},{16,160},{24,168},{32,144},{40,152},{48,128},{56,1... | collective-permute-start | bytes 3145736 | tf_op jit(solution)/shard_map/cond/branch_11_fun/ppermute | solution.py:449
  54.0 2.7 %collective-permute-start.15 = (f32[8,128,256]{2,1,0:T(8,128)S(1)}, f32[8,128,256]{2,1,0:T(8,128)S(1)}, u32[]{:S(2)}, u32[]{:S(2)}) collective-permute-start(f32[8,128,256]{2,1,0:T(8,128)S(1)} %param.17), channel_id=1, source_target_pairs={{0,8},{8,0},{16,24},{24,16},{32,40},{40,32},{48,56},{56,48},{64,72... | collective-permute-start | bytes 3145736 | tf_op jit(solution)/shard_map/cond/branch_1_fun/ppermute | solution.py:460
  57.7 9.7 %collective-permute-start.16 = (f32[128,256]{1,0:T(8,128)S(1)}, f32[128,256]{1,0:T(8,128)S(1)}, u32[]{:S(2)}, u32[]{:S(2)}) collective-permute-start(f32[128,256]{1,0:T(8,128)S(1)} %get-tuple-element.385), channel_id=1, source_target_pairs={{0,2},{1,3},{2,4},{3,5},{4,6},{5,7},{6,0},{7,1},{8,10},{9,11},{10,... | collective-permute-start | bytes 393224 | tf_op jit(solution)/shard_map/ppermute | solution.py:432
  59.1 10.2 %collective-permute-start.17 = (f32[128,256]{1,0:T(8,128)S(1)}, f32[128,256]{1,0:T(8,128)S(1)}, u32[]{:S(2)}, u32[]{:S(2)}) collective-permute-start(f32[128,256]{1,0:T(8,128)S(1)} %get-tuple-element.386), channel_id=1, source_target_pairs={{0,4},{1,5},{2,6},{3,7},{4,0},{5,1},{6,2},{7,3},{8,12},{9,13},{10,... | collective-permute-start | bytes 393224 | tf_op jit(solution)/shard_map/ppermute | solution.py:432
  59.4 9.9 %collective-permute-start.18 = (f32[128,256]{1,0:T(8,128)S(1)}, f32[128,256]{1,0:T(8,128)S(1)}, u32[]{:S(2)}, u32[]{:S(2)}) collective-permute-start(f32[128,256]{1,0:T(8,128)S(1)} %get-tuple-element.387), channel_id=1, source_target_pairs={{0,6},{1,7},{2,0},{3,1},{4,2},{5,3},{6,4},{7,5},{8,14},{9,15},{10,... | collective-permute-start | bytes 393224 | tf_op jit(solution)/shard_map/ppermute | solution.py:432
  61.9 7.5 %copy-start = (f32[2048,256]{1,0:T(8,128)S(1)}, f32[2048,256]{1,0:T(8,128)}, u32[]{:S(2)}) copy-start(f32[2048,256]{1,0:T(8,128)} %param.24) | copy-start | bytes 6291460
  61.9 10.9 %copy-start.2 = (bf16[4,1024,256]{2,1,0:T(8,128)(2,1)S(1)}, bf16[4,1024,256]{2,1,0:T(8,128)(2,1)}, u32[]{:S(2)}) copy-start(bf16[4,1024,256]{2,1,0:T(8,128)(2,1)} %get-tuple-element.389.later) | copy-start | bytes 6291460
  64.5 8.3 %copy-start.1 = (f32[8,256,256]{2,1,0:T(8,128)S(1)}, f32[8,256,256]{2,1,0:T(8,128)}, u32[]{:S(2)}) copy-start(f32[8,256,256]{2,1,0:T(8,128)} %get-tuple-element.388.sums) | copy-start | bytes 6291460
  64.6 20.9 %collective-permute-start.23 = (f32[256,256]{1,0:T(8,128)S(1)}, f32[256,256]{1,0:T(8,128)S(1)}, u32[]{:S(2)}, u32[]{:S(2)}) collective-permute-start(f32[256,256]{1,0:T(8,128)S(1)} %get-tuple-element.401), channel_id=1, source_target_pairs={{0,2},{1,3},{2,4},{3,5},{4,6},{5,7},{6,0},{7,1},{8,10},{9,11},{10,... | collective-permute-start | bytes 786440 | tf_op jit(solution)/shard_map/ppermute | solution.py:432
  64.7 21.4 %collective-permute-start.24 = (f32[256,256]{1,0:T(8,128)S(1)}, f32[256,256]{1,0:T(8,128)S(1)}, u32[]{:S(2)}, u32[]{:S(2)}) collective-permute-start(f32[256,256]{1,0:T(8,128)S(1)} %get-tuple-element.402), channel_id=1, source_target_pairs={{0,4},{1,5},{2,6},{3,7},{4,0},{5,1},{6,2},{7,3},{8,12},{9,13},{10,... | collective-permute-start | bytes 786440 | tf_op jit(solution)/shard_map/ppermute | solution.py:432
  67.4 18.6 %collective-permute-start.25 = (f32[256,256]{1,0:T(8,128)S(1)}, f32[256,256]{1,0:T(8,128)S(1)}, u32[]{:S(2)}, u32[]{:S(2)}) collective-permute-start(f32[256,256]{1,0:T(8,128)S(1)} %get-tuple-element.403), channel_id=1, source_target_pairs={{0,6},{1,7},{2,0},{3,1},{4,2},{5,3},{6,4},{7,5},{8,14},{9,15},{10,... | collective-permute-start | bytes 786440 | tf_op jit(solution)/shard_map/ppermute | solution.py:432
  70.1 10.6 %collective-permute-start.19 = (f32[128,256]{1,0:T(8,128)S(1)}, f32[128,256]{1,0:T(8,128)S(1)}, u32[]{:S(2)}, u32[]{:S(2)}) collective-permute-start(f32[128,256]{1,0:T(8,128)S(1)} %shard_map.88.mine), channel_id=1, source_target_pairs={{0,1},{1,0},{2,3},{3,2},{4,5},{5,4},{6,7},{7,6},{8,9},{9,8},{10,11... | collective-permute-start | bytes 393224 | tf_op jit(solution)/shard_map/ppermute | solution.py:437
  81.8 18.9 %collective-permute-start.20 = (f32[384,256]{1,0:T(8,128)S(1)}, f32[384,256]{1,0:T(8,128)S(1)}, u32[]{:S(2)}, u32[]{:S(2)}) collective-permute-start(f32[384,256]{1,0:T(8,128)S(1)} %get-tuple-element.397), channel_id=1, source_target_pairs={{0,2},{1,3},{2,4},{3,5},{4,6},{5,7},{6,0},{7,1},{8,10},{9,11},{10,... | collective-permute-start | bytes 1179656 | tf_op jit(solution)/shard_map/ppermute | solution.py:432
  81.9 20.9 %collective-permute-start.21 = (f32[384,256]{1,0:T(8,128)S(1)}, f32[384,256]{1,0:T(8,128)S(1)}, u32[]{:S(2)}, u32[]{:S(2)}) collective-permute-start(f32[384,256]{1,0:T(8,128)S(1)} %get-tuple-element.398), channel_id=1, source_target_pairs={{0,4},{1,5},{2,6},{3,7},{4,0},{5,1},{6,2},{7,3},{8,12},{9,13},{10,... | collective-permute-start | bytes 1179656 | tf_op jit(solution)/shard_map/ppermute | solution.py:432
  85.4 17.3 %collective-permute-start.22 = (f32[384,256]{1,0:T(8,128)S(1)}, f32[384,256]{1,0:T(8,128)S(1)}, u32[]{:S(2)}, u32[]{:S(2)}) collective-permute-start(f32[384,256]{1,0:T(8,128)S(1)} %get-tuple-element.399), channel_id=1, source_target_pairs={{0,6},{1,7},{2,0},{3,1},{4,2},{5,3},{6,4},{7,5},{8,14},{9,15},{10,... | collective-permute-start | bytes 1179656 | tf_op jit(solution)/shard_map/ppermute | solution.py:432
  86.1 14.6 %collective-permute-start.26 = (f32[256,256]{1,0:T(8,128)S(1)}, f32[256,256]{1,0:T(8,128)S(1)}, u32[]{:S(2)}, u32[]{:S(2)}) collective-permute-start(f32[256,256]{1,0:T(8,128)S(1)} %add_add_fusion), channel_id=1, source_target_pairs={{0,1},{1,0},{2,3},{3,2},{4,5},{5,4},{6,7},{7,6},{8,9},{9,8},{10,11... | collective-permute-start | bytes 786440 | tf_op jit(solution)/shard_map/ppermute | solution.py:437

commit v2 on v1

--- a/solution.py
+++ b/solution.py
@@ -317,7 +317,7 @@
     )(slots, hot, in_vmem(kept), in_vmem(incoming))
 
 
-def hot_pick_kernel(slots, hot, table, incoming, in1, in2, in3, out, sem):
+def hot_pick_kernel(slots, hot, table, incoming, in1, in3, in2, out, sem):
     x = lax.axis_index("rep") // 2
     owner_x = hot[0, x] // (2 * BLK_DEV)
     behind = lax.rem(x - owner_x + N_X, N_X)
@@ -349,7 +349,7 @@
         scratch_shapes=[pltpu.SemaphoreType.DMA((1,))],
         compiler_params=params(8),
         cost_estimate=cost(0, 2**18),
-    )(slots, hot, blocks, in_vmem(incoming), *pieces)
+    )(slots, hot, blocks, in_vmem(incoming), *[pieces[n] for n in (0, 2, 1)])
 
 
 def table_kernel(slots, table, incoming, out, came, sems):
@@ -394,7 +394,7 @@
     )(slots, blocks, incoming)
 
 
-def finish_kernel(counts, hot, in0, in1, in2, in3, other, pooled, hot_cache, sems):
+def finish_kernel(counts, hot, in0, in1, in3, in2, other, pooled, hot_cache, sems):
     rep = lax.axis_index("rep")
     x = rep // 2
     blocks = (hot, in1.at[E:], in2.at[E:], in3.at[E:])
@@ -421,7 +421,7 @@
         scratch_shapes=[pltpu.SemaphoreType.DMA((N_X,))],
         compiler_params=params(16),
         cost_estimate=cost(2**19, 2**21),
-    )(counts, hot, *pieces, other)
+    )(counts, hot, *[pieces[n] for n in (0, 1, 3, 2)], other)
 
 
 def ahead_by(step):
@@ -467,7 +467,7 @@
     hot_mine = hot_pick(swap_slots, hot_ids, blocks, incoming, hot_pieces)
     own, *homeward = home(sums, later_home, parts)
     *homeward, hot_block = add_hot(hot_ids, hot_mine, other_side(hot_mine), homeward)
-    crossing = other_side(away[0] + away[1] + away[2] + away[3])
+    crossing = other_side(away[0] + away[1] + away[3] + away[2])
     homeward = to_all_x([own, *homeward])
     after = table_after(swap_slots, blocks, incoming)
     pooled, hot_cache = finish(req_count, hot_block, homeward, crossing)

time: 105 us -> 102 us (0.971); the launches traced: 105 us -> 103 us
  waiting for transfers between devices: 27.7 us -> 19.8 us
  starting transfers between devices: 22.9 us -> 29.6 us
    ppermute x2, waiting for transfers between devices: 16.6 us -> 10.2 us  [other_side(): return lax.ppermute(value, 'rep', [(r, r ^ 1) for r in range(N_REP)])]
    ppermute x2, starting transfers between devices: 5.04 us -> 10.1 us  [other_side(): return lax.ppermute(value, 'rep', [(r, r ^ 1) for r in range(N_REP)])]
    ppermute x9, starting transfers between devices: 13.2 us -> 14.9 us  [to_all_x(): moved = {n: lax.ppermute(pieces[n], 'rep', ahead_by(n)) for n in (2, 1, 3)}]
    ppermute x1, waiting for transfers between devices: 6.35 us -> 5.15 us  [branch(): lax.ppermute(leaving, 'shard', [(s, s ^ mask * 2) for s in range(N_SHARD)])]
  transfers between devices with their start and end apart: 13 -> 13, of which waited for: 5 -> 5; matrix products, arithmetic and copies ran while one was open for 0% -> 0% of each run, Pallas kernels for 45% -> 46%
where the time goes in v2:
time: 102 us; the launch traced here: 103 us
  Pallas kernels  51.7 us (51%)
  starting transfers between devices  29.6 us (29%)
  waiting for transfers between devices  19.8 us (19%)
  between operations  1.7 us (2%)
    pallas_call x1, Pallas kernels, early(): pl.pallas_call(early_kernel, out_shape=(f32(PIECES, E, OWN), jax.ShapeDty...  39.3 us
    ppermute x9, starting transfers between devices, to_all_x(): moved = {n: lax.ppermute(pieces[n], 'rep', ahead_by(n)) for n in (2, 1, 3)}  14.9 us
    ppermute x2, waiting for transfers between devices, other_side(): return lax.ppermute(value, 'rep', [(r, r ^ 1) for r in range(N_REP)])  10.2 us
    ppermute x2, starting transfers between devices, other_side(): return lax.ppermute(value, 'rep', [(r, r ^ 1) for r in range(N_REP)])  10.1 us
    ppermute x1, waiting for transfers between devices, branch(): lax.ppermute(leaving, 'shard', [(s, s ^ mask * 2) for s in range(N_SHARD)])  5.15 us
    ppermute x1, starting transfers between devices, branch(): lax.ppermute(leaving, 'shard', [(s, s ^ mask * 2) for s in range(N_SHARD)])  4.37 us
    ppermute x1, waiting for transfers between devices, body(): lax.ppermute(value, 'shard', [(s, s ^ 1) for s in range(N_SHARD)])  2.64 us
    pallas_call x1, Pallas kernels, late(): pl.pallas_call(late_kernel, out_shape=(f32(E, OWN),) * N_X + (jax.ShapeDt...  2.63 us
  transfers between devices with their start and end apart: 13, of which 5 were waited for; matrix products, arithmetic and copies ran while one was open for 0% of the time, Pallas kernels for 46%

profile of v2, /device:TPU:32, one launch (start us, length us, event | category | flops | bytes accessed | tf_op | source)
XLA Modules:
  0.0 103.3 jit_solution(14617866185284003380)
XLA Ops:
  0.6 0.0 copy-start.4
  0.6 0.0 copy-start.5
  0.7 0.0 copy-start.3
  1.3 2.0 %shard_map.85 = f32[8,128,256]{2,1,0:T(8,128)S(1)} custom-call(s32[1,8]{1,0:T(1,128)} %slots.7, f32[16,128,256]{2,1,0:T(8,128)} %bitcast.12), custom_call_target="tpu_custom_call" | custom-call | bytes 2097152 | tf_op jit(solution)/shard_map/pallas_call | solution.py:66
  3.4 0.0 copy-done.4
  3.4 0.0 copy-done.5
  3.4 0.0 copy-done.3
  3.4 49.1 %conditional.2 = (f32[8,128,256]{2,1,0:T(8,128)S(1)}, f32[8,256,256]{2,1,0:T(8,128)}, bf16[4,1024,256]{2,1,0:T(8,128)(2,1)S(1)}, bf16[4,1024,256]{2,1,0:T(8,128)(2,1)}, f32[3,128,256]{2,1,0:T(8,128)S(1)}) conditional(s32[]{:T(128)} %clamp.3, (s32[1,8]{1,0:T(1,128)S(1)}, s32[1,4]{1,0:T(1,128)S(1)}, ...), branch_computations={%region_0.1_spmd, %region_1.2_spmd, %region_2.3_spmd, %region_3.4_... | conditional | flops 17179869184 | bytes 39845968 | solution.py:453
  3.5 4.4 %collective-permute-start.5 = (f32[8,128,256]{2,1,0:T(8,128)S(1)}, f32[8,128,256]{2,1,0:T(8,128)S(1)}, u32[]{:S(2)}, u32[]{:S(2)}) collective-permute-start(f32[8,128,256]{2,1,0:T(8,128)S(1)} %get-tuple-element.257), channel_id=1, source_target_pairs={{0,96},{8,104},{16,112},{24,120},{32,64},{40,72},{48,80},{56,88},{... | collective-permute-start | bytes 3145736 | tf_op jit(solution)/shard_map/cond/branch_6_fun/ppermute | solution.py:449
  7.9 39.3 %branch_6_fun.1 = (f32[8,256,256]{2,1,0:T(8,128)}, bf16[4,1024,256]{2,1,0:T(8,128)(2,1)S(1)}, bf16[4,1024,256]{2,1,0:T(8,128)(2,1)}, f32[3,128,256]{2,1,0:T(8,128)S(1)}) custom-call(s32[1,8]{1,0:T(1,128)S(1)} %get-tuple-element.258.slots, s32[1,4]{1,0:T(1,128)S(1)} %get-tuple-element.259.hot, s32[16,2048]{1,0:T(8,128)} %get-tuple-element.260.raw_keys, ...), custom_call_target="tpu_custom_call" | custom-call | flops 17179869184 | bytes 33554432 | tf_op jit(solution)/shard_map/cond/branch_6_fun/pallas_call | solution.py:185
  47.1 5.2 %collective-permute-done.5 = f32[8,128,256]{2,1,0:T(8,128)S(1)} collective-permute-done((f32[8,128,256]{2,1,0:T(8,128)S(1)}, f32[8,128,256]{2,1,0:T(8,128)S(1)}, u32[]{:S(2)}, u32[]{:S(2)}) %collective-permute-start.5) | collective-permute-done | bytes 1048608 | tf_op jit(solution)/shard_map/cond/branch_6_fun/ppermute | solution.py:449
  52.3 0.1 copy.42
  52.6 2.8 %conditional.3 = (f32[8,128,256]{2,1,0:T(8,128)S(1)}) conditional(s32[]{:T(128)} %convert_element_type.3, f32[8,128,256]{2,1,0:T(8,128)S(1)} %get-tuple-element.383, f32[8,128,256]{2,1,0:T(8,128)S(1)} %get-tuple-element.383), branch_computations={%region_16.17_spmd, %region_17.18_spmd} | conditional | bytes 6291504 | solution.py:458
  52.6 0.1 collective-permute-start.15
  52.7 2.6 %collective-permute-done.15 = f32[8,128,256]{2,1,0:T(8,128)S(1)} collective-permute-done((f32[8,128,256]{2,1,0:T(8,128)S(1)}, f32[8,128,256]{2,1,0:T(8,128)S(1)}, u32[]{:S(2)}, u32[]{:S(2)}) %collective-permute-start.15) | collective-permute-done | bytes 1048608 | tf_op jit(solution)/shard_map/cond/branch_1_fun/ppermute | solution.py:460
  55.3 0.1 copy.93
  55.4 0.9 shard_map.87
  56.3 0.1 collective-permute-start.16
  56.4 3.2 %collective-permute-start.17 = (f32[128,256]{1,0:T(8,128)S(1)}, f32[128,256]{1,0:T(8,128)S(1)}, u32[]{:S(2)}, u32[]{:S(2)}) collective-permute-start(f32[128,256]{1,0:T(8,128)S(1)} %get-tuple-element.386), channel_id=1, source_target_pairs={{0,6},{1,7},{2,0},{3,1},{4,2},{5,3},{6,4},{7,5},{8,14},{9,15},{10,... | collective-permute-start | bytes 393224 | tf_op jit(solution)/shard_map/ppermute | solution.py:432
  59.6 3.1 %collective-permute-start.18 = (f32[128,256]{1,0:T(8,128)S(1)}, f32[128,256]{1,0:T(8,128)S(1)}, u32[]{:S(2)}, u32[]{:S(2)}) collective-permute-start(f32[128,256]{1,0:T(8,128)S(1)} %get-tuple-element.387), channel_id=1, source_target_pairs={{0,4},{1,5},{2,6},{3,7},{4,0},{5,1},{6,2},{7,3},{8,12},{9,13},{10,... | collective-permute-start | bytes 393224 | tf_op jit(solution)/shard_map/ppermute | solution.py:432
  62.7 0.0 copy-start
  62.7 0.0 copy-start.2
  62.7 2.6 %shard_map.89 = (f32[256,256]{1,0:T(8,128)S(1)}, f32[256,256]{1,0:T(8,128)S(1)}, f32[256,256]{1,0:T(8,128)S(1)}, f32[256,256]{1,0:T(8,128)S(1)}, bf16[512,1024]{1,0:T(8,128)(2,1)S(1)}) custom-call(f32[8,256,256]{2,1,0:T(8,128)} %get-tuple-element.388.sums, bf16[4,1024,256]{2,1,0:T(8,128)(2,1)S(1)} %get-tuple-element.390.later, ...), custom_call_target="tpu_custom_call" | custom-call | flops 1073741824 | bytes 4194304 | tf_op jit(solution)/shard_map/pallas_call | solution.py:221
  65.3 0.0 copy-start.1
  65.4 0.1 collective-permute-start.23
  65.4 3.2 %collective-permute-start.24 = (f32[256,256]{1,0:T(8,128)S(1)}, f32[256,256]{1,0:T(8,128)S(1)}, u32[]{:S(2)}, u32[]{:S(2)}) collective-permute-start(f32[256,256]{1,0:T(8,128)S(1)} %get-tuple-element.402), channel_id=1, source_target_pairs={{0,6},{1,7},{2,0},{3,1},{4,2},{5,3},{6,4},{7,5},{8,14},{9,15},{10,... | collective-permute-start | bytes 786440 | tf_op jit(solution)/shard_map/ppermute | solution.py:432
  68.7 0.0 collective-permute-done.16.in1
  68.7 0.0 collective-permute-start.25
  68.7 0.0 collective-permute-done.17.in3
  68.7 0.0 collective-permute-done.18.in2
  68.7 0.0 copy-done
  68.7 0.7 shard_map.88.mine
  69.4 5.9 %collective-permute-start.19 = (f32[128,256]{1,0:T(8,128)S(1)}, f32[128,256]{1,0:T(8,128)S(1)}, u32[]{:S(2)}, u32[]{:S(2)}) collective-permute-start(f32[128,256]{1,0:T(8,128)S(1)} %shard_map.88.mine), channel_id=1, source_target_pairs={{0,1},{1,0},{2,3},{3,2},{4,5},{5,4},{6,7},{7,6},{8,9},{9,8},{10,11... | collective-permute-start | bytes 393224 | tf_op jit(solution)/shard_map/ppermute | solution.py:437
  75.3 0.0 copy-done.2
  75.3 0.0 copy-done.1
  75.3 1.3 %shard_map.90 = (f32[256,256]{1,0:T(8,128)S(1)}, f32[384,256]{1,0:T(8,128)S(1)}, f32[384,256]{1,0:T(8,128)S(1)}, f32[384,256]{1,0:T(8,128)S(1)}) custom-call(f32[8,256,256]{2,1,0:T(8,128)S(1)} %copy-done.1, bf16[4,1024,256]{2,1,0:T(8,128)(2,1)S(1)} %copy-done.2, bf16[512,1024]{1,0:T(8,128)(2,1)S(1)} %get-tuple-element.391.parts), custom_call_target="tpu_custom_call" | custom-call | flops 1073741824 | bytes 4194304 | tf_op jit(solution)/shard_map/pallas_call | solution.py:242
  76.6 3.7 %collective-permute-done.19.other = f32[128,256]{1,0:T(8,128)S(1)} collective-permute-done((f32[128,256]{1,0:T(8,128)S(1)}, f32[128,256]{1,0:T(8,128)S(1)}, u32[]{:S(2)}, u32[]{:S(2)}) %collective-permute-start.19) | collective-permute-done | bytes 131104 | tf_op jit(solution)/shard_map/ppermute | solution.py:437
  80.3 1.1 %shard_map.91 = (f32[384,256]{1,0:T(8,128)S(1)}, f32[384,256]{1,0:T(8,128)S(1)}, f32[384,256]{1,0:T(8,128)S(1)}, f32[128,256]{1,0:T(8,128)S(1)}) custom-call(s32[1,4]{1,0:T(1,128)S(1)} %copy-done.5, f32[128,256]{1,0:T(8,128)S(1)} %shard_map.88.mine, ...), custom_call_target="tpu_custom_call", output_to_operand_aliasing={{0}: (3, {}), {1}: (4, {}), {2}: (5, {})} | custom-call | bytes 524288 | tf_op jit(solution)/shard_map/pallas_call | solution.py:276
  81.5 1.0 %collective-permute-start.20 = (f32[384,256]{1,0:T(8,128)S(1)}, f32[384,256]{1,0:T(8,128)S(1)}, u32[]{:S(2)}, u32[]{:S(2)}) collective-permute-start(f32[384,256]{1,0:T(8,128)S(1)} %get-tuple-element.397), channel_id=1, source_target_pairs={{0,2},{1,3},{2,4},{3,5},{4,6},{5,7},{6,0},{7,1},{8,10},{9,11},{10,... | collective-permute-start | bytes 1179656 | tf_op jit(solution)/shard_map/ppermute | solution.py:432
  82.5 2.3 %collective-permute-start.21 = (f32[384,256]{1,0:T(8,128)S(1)}, f32[384,256]{1,0:T(8,128)S(1)}, u32[]{:S(2)}, u32[]{:S(2)}) collective-permute-start(f32[384,256]{1,0:T(8,128)S(1)} %get-tuple-element.398), channel_id=1, source_target_pairs={{0,6},{1,7},{2,0},{3,1},{4,2},{5,3},{6,4},{7,5},{8,14},{9,15},{10,... | collective-permute-start | bytes 1179656 | tf_op jit(solution)/shard_map/ppermute | solution.py:432
  84.8 0.0 collective-permute-done.23
  84.8 1.9 %collective-permute-start.22 = (f32[384,256]{1,0:T(8,128)S(1)}, f32[384,256]{1,0:T(8,128)S(1)}, u32[]{:S(2)}, u32[]{:S(2)}) collective-permute-start(f32[384,256]{1,0:T(8,128)S(1)} %get-tuple-element.399), channel_id=1, source_target_pairs={{0,4},{1,5},{2,6},{3,7},{4,0},{5,1},{6,2},{7,3},{8,12},{9,13},{10,... | collective-permute-start | bytes 1179656 | tf_op jit(solution)/shard_map/ppermute | solution.py:432
  86.7 0.0 collective-permute-done.24
  86.7 0.0 collective-permute-done.25
  86.7 0.1 add_add_fusion
  86.8 4.3 %collective-permute-start.26 = (f32[256,256]{1,0:T(8,128)S(1)}, f32[256,256]{1,0:T(8,128)S(1)}, u32[]{:S(2)}, u32[]{:S(2)}) collective-permute-start(f32[256,256]{1,0:T(8,128)S(1)} %add_add_fusion), channel_id=1, source_target_pairs={{0,1},{1,0},{2,3},{3,2},{4,5},{5,4},{6,7},{7,6},{8,9},{9,8},{10,11... | collective-permute-start | bytes 786440 | tf_op jit(solution)/shard_map/ppermute | solution.py:437
  91.0 2.2 %shard_map.86 = f32[16,128,256]{2,1,0:T(8,128)} custom-call(s32[1,8]{1,0:T(1,128)S(1)} %copy-done.4, f32[16,128,256]{2,1,0:T(8,128)S(1)} %bitcast.30, f32[8,128,256]{2,1,0:T(8,128)S(1)} %get-tuple-element.486.incoming), custom_call_target="tpu_custom_call" | custom-call | bytes 4194304 | tf_op jit(solution)/shard_map/pallas_call | solution.py:386
  93.2 6.4 %collective-permute-done.26.other = f32[256,256]{1,0:T(8,128)S(1)} collective-permute-done((f32[256,256]{1,0:T(8,128)S(1)}, f32[256,256]{1,0:T(8,128)S(1)}, u32[]{:S(2)}, u32[]{:S(2)}) %collective-permute-start.26) | collective-permute-done | bytes 262176 | tf_op jit(solution)/shard_map/ppermute | solution.py:437
  99.7 0.0 collective-permute-done.20.in1
  99.7 0.0 collective-permute-done.21.in3
  99.7 1.8 %collective-permute-done.22.in2 = f32[384,256]{1,0:T(8,128)S(1)} collective-permute-done((f32[384,256]{1,0:T(8,128)S(1)}, f32[384,256]{1,0:T(8,128)S(1)}, u32[]{:S(2)}, u32[]{:S(2)}) %collective-permute-start.22) | collective-permute-done | bytes 393248 | tf_op jit(solution)/shard_map/ppermute | solution.py:432
  101.5 1.6 %shard_map.92 = (f32[256,256]{1,0:T(8,128)}, f32[4,128,256]{2,1,0:T(8,128)}) custom-call(s32[1,2048]{1,0:T(1,128)S(1)} %copy-done.3, f32[128,256]{1,0:T(8,128)S(1)} %get-tuple-element.395.hot, f32[256,256]{1,0:T(8,128)S(1)} %get-tuple-element.396.in0, f32[384,256]{1,0:T(8,128)S(1)} %collective-permute-done.20.in1, ...), custom_call_target="tpu_custom_call" | custom-call | flops 524288 | bytes 2097152 | tf_op jit(solution)/shard_map/pallas_call | solution.py:416
Async XLA Ops:
  0.6 2.8 %copy-start.4 = (s32[1,8]{1,0:T(1,128)S(1)}, s32[1,8]{1,0:T(1,128)}, u32[]{:S(2)}) copy-start(s32[1,8]{1,0:T(1,128)} %slots.7) | copy-start | bytes 100
  0.6 2.8 %copy-start.5 = (s32[1,4]{1,0:T(1,128)S(1)}, s32[1,4]{1,0:T(1,128)}, u32[]{:S(2)}) copy-start(s32[1,4]{1,0:T(1,128)} %hot.5) | copy-start | bytes 52
  0.7 2.8 %copy-start.3 = (s32[1,2048]{1,0:T(1,128)S(1)}, s32[1,2048]{1,0:T(1,128)}, u32[]{:S(2)}) copy-start(s32[1,2048]{1,0:T(1,128)} %counts.1) | copy-start | bytes 24580
  3.5 48.8 %collective-permute-start.5 = (f32[8,128,256]{2,1,0:T(8,128)S(1)}, f32[8,128,256]{2,1,0:T(8,128)S(1)}, u32[]{:S(2)}, u32[]{:S(2)}) collective-permute-start(f32[8,128,256]{2,1,0:T(8,128)S(1)} %get-tuple-element.257), channel_id=1, source_target_pairs={{0,96},{8,104},{16,112},{24,120},{32,64},{40,72},{48,80},{56,88},{... | collective-permute-start | bytes 3145736 | tf_op jit(solution)/shard_map/cond/branch_6_fun/ppermute | solution.py:449
  52.6 2.7 %collective-permute-start.15 = (f32[8,128,256]{2,1,0:T(8,128)S(1)}, f32[8,128,256]{2,1,0:T(8,128)S(1)}, u32[]{:S(2)}, u32[]{:S(2)}) collective-permute-start(f32[8,128,256]{2,1,0:T(8,128)S(1)} %param.17), channel_id=1, source_target_pairs={{0,8},{8,0},{16,24},{24,16},{32,40},{40,32},{48,56},{56,48},{64,72... | collective-permute-start | bytes 3145736 | tf_op jit(solution)/shard_map/cond/branch_1_fun/ppermute | solution.py:460
  56.3 12.4 %collective-permute-start.16 = (f32[128,256]{1,0:T(8,128)S(1)}, f32[128,256]{1,0:T(8,128)S(1)}, u32[]{:S(2)}, u32[]{:S(2)}) collective-permute-start(f32[128,256]{1,0:T(8,128)S(1)} %get-tuple-element.385), channel_id=1, source_target_pairs={{0,2},{1,3},{2,4},{3,5},{4,6},{5,7},{6,0},{7,1},{8,10},{9,11},{10,... | collective-permute-start | bytes 393224 | tf_op jit(solution)/shard_map/ppermute | solution.py:432
  56.4 12.3 %collective-permute-start.17 = (f32[128,256]{1,0:T(8,128)S(1)}, f32[128,256]{1,0:T(8,128)S(1)}, u32[]{:S(2)}, u32[]{:S(2)}) collective-permute-start(f32[128,256]{1,0:T(8,128)S(1)} %get-tuple-element.386), channel_id=1, source_target_pairs={{0,6},{1,7},{2,0},{3,1},{4,2},{5,3},{6,4},{7,5},{8,14},{9,15},{10,... | collective-permute-start | bytes 393224 | tf_op jit(solution)/shard_map/ppermute | solution.py:432
  59.6 9.1 %collective-permute-start.18 = (f32[128,256]{1,0:T(8,128)S(1)}, f32[128,256]{1,0:T(8,128)S(1)}, u32[]{:S(2)}, u32[]{:S(2)}) collective-permute-start(f32[128,256]{1,0:T(8,128)S(1)} %get-tuple-element.387), channel_id=1, source_target_pairs={{0,4},{1,5},{2,6},{3,7},{4,0},{5,1},{6,2},{7,3},{8,12},{9,13},{10,... | collective-permute-start | bytes 393224 | tf_op jit(solution)/shard_map/ppermute | solution.py:432
  62.7 6.0 %copy-start = (f32[2048,256]{1,0:T(8,128)S(1)}, f32[2048,256]{1,0:T(8,128)}, u32[]{:S(2)}) copy-start(f32[2048,256]{1,0:T(8,128)} %param.24) | copy-start | bytes 6291460
  62.7 12.6 %copy-start.2 = (bf16[4,1024,256]{2,1,0:T(8,128)(2,1)S(1)}, bf16[4,1024,256]{2,1,0:T(8,128)(2,1)}, u32[]{:S(2)}) copy-start(bf16[4,1024,256]{2,1,0:T(8,128)(2,1)} %get-tuple-element.389.later) | copy-start | bytes 6291460
  65.3 9.9 %copy-start.1 = (f32[8,256,256]{2,1,0:T(8,128)S(1)}, f32[8,256,256]{2,1,0:T(8,128)}, u32[]{:S(2)}) copy-start(f32[8,256,256]{2,1,0:T(8,128)} %get-tuple-element.388.sums) | copy-start | bytes 6291460
  65.4 19.4 %collective-permute-start.23 = (f32[256,256]{1,0:T(8,128)S(1)}, f32[256,256]{1,0:T(8,128)S(1)}, u32[]{:S(2)}, u32[]{:S(2)}) collective-permute-start(f32[256,256]{1,0:T(8,128)S(1)} %get-tuple-element.401), channel_id=1, source_target_pairs={{0,2},{1,3},{2,4},{3,5},{4,6},{5,7},{6,0},{7,1},{8,10},{9,11},{10,... | collective-permute-start | bytes 786440 | tf_op jit(solution)/shard_map/ppermute | solution.py:432
  65.4 21.3 %collective-permute-start.24 = (f32[256,256]{1,0:T(8,128)S(1)}, f32[256,256]{1,0:T(8,128)S(1)}, u32[]{:S(2)}, u32[]{:S(2)}) collective-permute-start(f32[256,256]{1,0:T(8,128)S(1)} %get-tuple-element.402), channel_id=1, source_target_pairs={{0,6},{1,7},{2,0},{3,1},{4,2},{5,3},{6,4},{7,5},{8,14},{9,15},{10,... | collective-permute-start | bytes 786440 | tf_op jit(solution)/shard_map/ppermute | solution.py:432
  68.7 18.0 %collective-permute-start.25 = (f32[256,256]{1,0:T(8,128)S(1)}, f32[256,256]{1,0:T(8,128)S(1)}, u32[]{:S(2)}, u32[]{:S(2)}) collective-permute-start(f32[256,256]{1,0:T(8,128)S(1)} %get-tuple-element.403), channel_id=1, source_target_pairs={{0,4},{1,5},{2,6},{3,7},{4,0},{5,1},{6,2},{7,3},{8,12},{9,13},{10,... | collective-permute-start | bytes 786440 | tf_op jit(solution)/shard_map/ppermute | solution.py:432
  69.4 10.9 %collective-permute-start.19 = (f32[128,256]{1,0:T(8,128)S(1)}, f32[128,256]{1,0:T(8,128)S(1)}, u32[]{:S(2)}, u32[]{:S(2)}) collective-permute-start(f32[128,256]{1,0:T(8,128)S(1)} %shard_map.88.mine), channel_id=1, source_target_pairs={{0,1},{1,0},{2,3},{3,2},{4,5},{5,4},{6,7},{7,6},{8,9},{9,8},{10,11... | collective-permute-start | bytes 393224 | tf_op jit(solution)/shard_map/ppermute | solution.py:437
  81.5 18.2 %collective-permute-start.20 = (f32[384,256]{1,0:T(8,128)S(1)}, f32[384,256]{1,0:T(8,128)S(1)}, u32[]{:S(2)}, u32[]{:S(2)}) collective-permute-start(f32[384,256]{1,0:T(8,128)S(1)} %get-tuple-element.397), channel_id=1, source_target_pairs={{0,2},{1,3},{2,4},{3,5},{4,6},{5,7},{6,0},{7,1},{8,10},{9,11},{10,... | collective-permute-start | bytes 1179656 | tf_op jit(solution)/shard_map/ppermute | solution.py:432
  82.5 17.2 %collective-permute-start.21 = (f32[384,256]{1,0:T(8,128)S(1)}, f32[384,256]{1,0:T(8,128)S(1)}, u32[]{:S(2)}, u32[]{:S(2)}) collective-permute-start(f32[384,256]{1,0:T(8,128)S(1)} %get-tuple-element.398), channel_id=1, source_target_pairs={{0,6},{1,7},{2,0},{3,1},{4,2},{5,3},{6,4},{7,5},{8,14},{9,15},{10,... | collective-permute-start | bytes 1179656 | tf_op jit(solution)/shard_map/ppermute | solution.py:432
  84.8 16.7 %collective-permute-start.22 = (f32[384,256]{1,0:T(8,128)S(1)}, f32[384,256]{1,0:T(8,128)S(1)}, u32[]{:S(2)}, u32[]{:S(2)}) collective-permute-start(f32[384,256]{1,0:T(8,128)S(1)} %get-tuple-element.399), channel_id=1, source_target_pairs={{0,4},{1,5},{2,6},{3,7},{4,0},{5,1},{6,2},{7,3},{8,12},{9,13},{10,... | collective-permute-start | bytes 1179656 | tf_op jit(solution)/shard_map/ppermute | solution.py:432
  86.8 12.9 %collective-permute-start.26 = (f32[256,256]{1,0:T(8,128)S(1)}, f32[256,256]{1,0:T(8,128)S(1)}, u32[]{:S(2)}, u32[]{:S(2)}) collective-permute-start(f32[256,256]{1,0:T(8,128)S(1)} %add_add_fusion), channel_id=1, source_target_pairs={{0,1},{1,0},{2,3},{3,2},{4,5},{5,4},{6,7},{7,6},{8,9},{9,8},{10,11... | collective-permute-start | bytes 786440 | tf_op jit(solution)/shard_map/ppermute | solution.py:437
